TPU v7x, 512 devices: a whole 4x4x16 slice. The times are simulated.
512 devices in a mesh: expert: 8 (over z_lo, core), ffn: 16 (over y, z_hi), section: 4 (over x).
Axes of the slice: x: 4, y: 4, z: 16 (z_hi: 4, z_lo: 4; z = z_hi * 4 + z_lo), core: 2. Of those that a mesh axis runs over, the one named last changes fastest.
Arguments:
- layer_input: bfloat16 [1024, 6144], P('expert', 'section'), may hold values from -6 to 6
- out_grad: bfloat16 [1024, 6144], P('expert', 'section'), may hold values from -6 to 6
- scores: bfloat16 [8, 384], P(None, 'expert'), may hold values from 0.049804688 to 1
- picks: int32 [8, 384], P(None, 'expert'), may hold values from 0 to 127, as said below
- w_gate: bfloat16 [8, 6144, 6144], P('expert', 'ffn', 'section'), may hold values from -0.078125 to 0.078125
- w_up: bfloat16 [8, 6144, 6144], P('expert', 'ffn', 'section'), may hold values from -0.078125 to 0.078125
- w_down: bfloat16 [8, 6144, 6144], P('expert', 'ffn', 'section'), may hold values from -0.078125 to 0.078125
Outputs:
- input_grad: bfloat16 [1024, 6144], P('expert', 'section')
- score_grad: bfloat16 [8, 384], P(None, 'expert')
Inputs may be any that keep to these rules, and one draw needn't show every extreme that they name: `picks`: in each row, the columns j * 48 to (j + 1) * 48 - 1 hold 48 different indices of tokens of the j-th shard of 128 tokens.
All inputs are finite; a program needn't handle non-finite values.
Results may differ from a plain program's by a relative error of at most 0.0057.
Values may be sent and summed in bfloat16 or wider, within the bound.
No kernel may reach another device: no remote copies, remote signals or barrier semaphores. Data moves between devices by JAX's collectives and lax.ppermute only.
A program may use at most 64 MiB of HBM per device.

v0:
```python
import jax
import jax.numpy as jnp
from jax import lax
from jax.sharding import PartitionSpec as P


def project(rows, weight):
    return lax.dot_general(
        rows, weight, (((1,), (1,)), ((), ())), preferred_element_type=jnp.float32
    )


def local(layer_input, out_grad, scores, picks, w_gate, w_up, w_down):
    num_experts = picks.shape[0]
    per_source = picks.shape[1]
    width = layer_input.shape[1]
    flat_picks = picks.reshape(-1)
    x_sel = jnp.take(layer_input, flat_picks, axis=0).reshape(num_experts, per_source, width)
    g_sel = jnp.take(out_grad, flat_picks, axis=0).reshape(num_experts, per_source, width)
    x_recv, g_recv, s_recv = (
        lax.all_to_all(x_sel, "expert", split_axis=0, concat_axis=1, tiled=True),
        lax.all_to_all(g_sel, "expert", split_axis=0, concat_axis=1, tiled=True),
        lax.all_to_all(scores, "expert", split_axis=0, concat_axis=1, tiled=True),
    )
    x_rows = x_recv[0]
    g_rows = g_recv[0]
    weight = s_recv[0].astype(jnp.float32)[:, None]
    gate_w = w_gate[0]
    up_w = w_up[0]
    gate_part = project(x_rows, gate_w)
    up_part = project(x_rows, up_w)
    back_part = project(g_rows, w_down[0])
    gate, up, back = lax.psum((gate_part, up_part, back_part), "section")
    sig = jax.nn.sigmoid(gate)
    act = gate * sig
    partial_score = jnp.sum(act * up * back, axis=1)
    grad_h = weight * back
    hidden_d_up = (grad_h * act).astype(jnp.bfloat16)
    hidden_d_gate = (grad_h * up * sig * (1.0 + gate * (1.0 - sig))).astype(jnp.bfloat16)
    partial_score, d_gate, d_up = (partial_score, hidden_d_gate, hidden_d_up)
    score_sum = lax.psum(partial_score, "ffn")
    first = lax.dot_general(
        gate_w, d_gate, (((0,), (1,)), ((), ())), preferred_element_type=jnp.float32
    )
    second = lax.dot_general(
        up_w, d_up, (((0,), (1,)), ((), ())), preferred_element_type=jnp.float32
    )
    grad_cols = lax.psum_scatter(first + second, "ffn", scatter_dimension=0, tiled=True)
    row_grad = grad_cols.astype(jnp.bfloat16)
    score_row = score_sum.astype(jnp.bfloat16).reshape(1, -1)
    back_grad, back_score = (
        lax.all_to_all(row_grad, "expert", split_axis=1, concat_axis=1, tiled=True),
        lax.all_to_all(score_row, "expert", split_axis=1, concat_axis=1, tiled=True),
    )
    tok_count = layer_input.shape[0]
    one_hot = (flat_picks[:, None] == jnp.arange(tok_count, dtype=jnp.int32)[None, :]).astype(
        jnp.bfloat16
    )
    token_grad = jnp.dot(back_grad, one_hot, preferred_element_type=jnp.float32)
    token_grad = token_grad.astype(jnp.bfloat16).T
    input_grad = lax.all_gather(token_grad, "ffn", axis=1, tiled=True)
    return (input_grad, back_score.reshape(num_experts, per_source))


def solution(mesh):
    placed = (
        P("expert", "section"),
        P("expert", "section"),
        P(None, "expert"),
        P(None, "expert"),
        P("expert", "ffn", "section"),
        P("expert", "ffn", "section"),
        P("expert", "ffn", "section"),
    )
    return jax.shard_map(
        local,
        mesh=mesh,
        in_specs=placed,
        out_specs=(P("expert", "section"), P(None, "expert")),
        check_vma=False,
    )
```

profile of v0, /device:TPU:2, one launch (start us, length us, event | category | flops | bytes accessed | tf_op | source)
XLA Modules:
  0.0 375.8 jit_solution(368176025021085568)
XLA Ops:
  7.2 0.9 eq.15
  8.1 4.8 %gather_fusion.1 = bf16[384,1536]{1,0:T(8,128)(2,1)S(1)} fusion(bf16[128,1536]{1,0:T(8,128)(2,1)} %param.9, s32[1024]{0:T(1024)S(1)} %pad_clamp_fusion), kind=kCustom, calls=%fused_computation.1.clone | custom fusion | bytes 2360832 | tf_op jit(solution)/shard_map/jit(_take)/gather | solution.py:18
  12.9 2.8 gather_fusion
  15.7 2.7 broadcast_select_fusion.1
  18.4 35.1 %all_to_all.53 = bf16[8,48,1536]{2,1,0:T(8,128)(2,1)S(1)} all-to-all(bf16[8,48,1536]{2,1,0:T(8,128)(2,1)S(1)} %bitcast.30), channel_id=1, replica_groups=mesh['expert'=8,'ffn'=16,'section'=4] {'expert'}, dimensions={0} | all-to-all | bytes 2359296 | tf_op jit(solution)/shard_map/all_to_all | solution.py:21
  53.5 3.6 all-to-all-start.1
  57.1 1.6 fusion.3
  58.7 1.6 fusion.6
  60.4 26.0 %all-to-all-done.1 = bf16[8,48,1536]{2,1,0:T(8,128)(2,1)S(1)} async-done(((bf16[8,48,1536]{2,1,0:T(8,128)(2,1)}), bf16[8,48,1536]{2,1,0:T(8,128)(2,1)S(1)}, u32[]{:S(2)}, u32[]{:S(2)}) %all-to-all-start.1) | async-done | bytes 1179680 | tf_op jit(solution)/shard_map/all_to_all | solution.py:22
  86.4 2.9 fusion.8
  89.3 0.6 copy-done.9
  89.9 7.9 %all_to_all.54 = bf16[8,1,48]{2,1,0:T(2,128)(2,1)S(1)} all-to-all(bf16[8,1,48]{2,1,0:T(2,128)(2,1)S(1)} %copy.11), channel_id=1, replica_groups=mesh['expert'=8,'ffn'=16,'section'=4] {'expert'}, dimensions={0} | all-to-all | bytes 1536 | tf_op jit(solution)/shard_map/all_to_all | solution.py:23
  97.9 0.1 reshape.52
  97.9 61.2 %all-reduce.3.cloned.1.call-done = (f32[384,384]{1,0:T(8,128)}, f32[384,384]{1,0:T(8,128)}, f32[384,384]{1,0:T(8,128)}) async-done(((f32[384,384]{1,0:T(8,128)}, f32[384,384]{1,0:T(8,128)}, f32[384,384]{1,0:T(8,128)}), (f32[384,384]{1,0:T(8,128)}, f32[384,384]{1,0:T(8,128)}, f32[384,384]{1,0:T(8,128)})) %all-reduce.3.cloned.1.call-update) | async-done | bytes 1769488 | tf_op jit(solution)/shard_map/psum | solution.py:33
  159.2 2.5 fusion.1
  161.7 0.9 fusion
  162.6 2.0 copy.14
  164.6 1.0 copy-done.3
  165.6 0.2 copy-done.5
  165.8 0.2 copy-done.6
  165.9 0.3 multiply_reduce_fusion
  166.2 56.3 %psum.31 = bf16[384]{0:T(512)(128)(2,1)S(1)} all-reduce(f32[384]{0:T(512)S(1)} %multiply_reduce_fusion), channel_id=1, replica_groups=mesh['expert'=8,'ffn'=16,'section'=4] {'ffn'}, use_global_device_ids=true, to_apply=%region_5.7 | all-reduce | flops 384 | bytes 2304 | tf_op jit(solution)/shard_map/psum | solution.py:41
  222.5 0.7 all_to_all.47
  223.1 3.3 all-to-all-start.4
  226.4 75.5 %reduce-scatter.4.cloned.1.call-done = f32[96,384]{1,0:T(8,128)} async-done(((f32[1536,384]{1,0:T(8,128)}), f32[96,384]{1,0:T(8,128)}) %reduce-scatter.4.cloned.1.call-update) | async-done | bytes 147472
  302.0 1.7 copy.15
  303.6 3.4 all-to-all-start.3
  307.0 0.6 copy.18
  307.6 5.7 %all-to-all-done.3 = bf16[96,8,48]{0,2,1:T(8,128)(2,1)S(1)} async-done(((bf16[96,8,48]{0,2,1:T(8,128)(2,1)}), bf16[96,8,48]{0,2,1:T(8,128)(2,1)S(1)}, u32[]{:S(2)}, u32[]{:S(2)}) %all-to-all-start.3) | async-done | bytes 73760 | tf_op jit(solution)/shard_map/all_to_all | solution.py:52
  313.3 0.3 convolution_convert_fusion
  313.5 54.5 %all_gather.3 = bf16[128,1536]{0,1:T(8,128)(2,1)S(1)} all-gather(bf16[128,96]{0,1:T(8,128)(2,1)S(1)} %convolution_convert_fusion), channel_id=1, replica_groups=mesh['expert'=8,'ffn'=16,'section'=4] {'ffn'}, dimensions={1}, use_global_device_ids=true | all-gather | bytes 417792 | tf_op jit(solution)/shard_map/all_gather | solution.py:61
  368.1 0.9 copy.13
  (26 shorter events, 0.2 us)
Async XLA Ops:
  7.2 49.9 %copy-start = (bf16[1,384,1536]{2,1,0:T(8,128)(2,1)S(1)}, bf16[1,384,1536]{2,1,0:T(8,128)(2,1)}, u32[]{:S(2)}) copy-start(bf16[1,384,1536]{2,1,0:T(8,128)(2,1)} %param.13) | copy-start | bytes 3538948
  8.1 4.8 %copy-start.1 = (bf16[128,1536]{1,0:T(8,128)(2,1)S(1)}, bf16[128,1536]{1,0:T(8,128)(2,1)}, u32[]{:S(2)}) copy-start(bf16[128,1536]{1,0:T(8,128)(2,1)} %param.10) | copy-start | bytes 1179652
  53.5 32.9 %all-to-all-start.1 = ((bf16[8,48,1536]{2,1,0:T(8,128)(2,1)}), bf16[8,48,1536]{2,1,0:T(8,128)(2,1)S(1)}, u32[]{:S(2)}, u32[]{:S(2)}) async-start(bf16[8,48,1536]{2,1,0:T(8,128)(2,1)} %bitcast.1), calls=%async_computation.1 | async-start | bytes 2359296 | tf_op jit(solution)/shard_map/all_to_all | solution.py:22
  57.0 102.1 %all-reduce.3.cloned.1.call-start = ((), (), s32[]{:S(2)}) async-start(), calls=%async_computation.7 | async-start | bytes 3538944 | tf_op jit(solution)/shard_map/psum | solution.py:33
  57.1 1.7 copy-start.7
  89.2 0.7 copy-start.9
  89.3 212.7 %reduce-scatter.4.cloned.1.call-start = ((), (), s32[]{:S(2)}) async-start(), calls=%async_computation.6 | async-start | bytes 2506752
  159.2 2.5 copy-start.2
  159.2 2.5 copy-start.4
  159.2 2.5 copy-start.8
  164.5 1.1 copy-start.3
  164.5 1.2 copy-start.5
  164.5 1.4 copy-start.6
  223.1 80.5 %all-to-all-start.4 = ((bf16[1,8,48]{2,0,1:T(2,128)(2,1)}), bf16[1,8,48]{2,0,1:T(2,128)(2,1)S(1)}, u32[]{:S(2)}, u32[]{:S(2)}) async-start(bf16[1,8,48]{2,0,1:T(2,128)(2,1)} %all_to_all.47), calls=%async_computation.4 | async-start | bytes 8192 | tf_op jit(solution)/shard_map/all_to_all | solution.py:53
  303.6 9.6 %all-to-all-start.3 = ((bf16[96,8,48]{0,2,1:T(8,128)(2,1)}), bf16[96,8,48]{0,2,1:T(8,128)(2,1)S(1)}, u32[]{:S(2)}, u32[]{:S(2)}) async-start(bf16[96,8,48]{0,2,1:T(8,128)(2,1)} %bitcast.9), calls=%async_computation.3 | async-start | bytes 196608 | tf_op jit(solution)/shard_map/all_to_all | solution.py:52
Sparse Core Ops, SparseCore 0:
  89.4 69.7 all-reduce.2
  164.7 137.2 reduce-scatter.3
where the time goes:
time: 377 us; the launch traced here: 376 us
  waiting for transfers between devices  168 us (45%)
  blocking collectives  154 us (41%)
  local copies, waits for them, and re-layouts  16.4 us (4%)
  between operations  14.2 us (4%)
  starting transfers between devices  10.3 us (3%)
  matrix products  9.75 us (3%)
    unnamed x3, waiting for transfers between devices  75.6 us
    psum x1, waiting for transfers between devices, local(): gate, up, back = lax.psum((gate_part, up_part, back_part), 'section')  61.2 us
    psum x1, blocking collectives, local(): score_sum = lax.psum(partial_score, 'ffn')  56.3 us
    all_gather x1, blocking collectives, local(): input_grad = lax.all_gather(token_grad, 'ffn', axis=1, tiled=True)  54.5 us
    all_to_all x1, blocking collectives, local(): lax.all_to_all(x_sel, 'expert', split_axis=0, concat_axis=1, tiled=True)  35.1 us
    all_to_all x1, waiting for transfers between devices, local(): lax.all_to_all(g_sel, 'expert', split_axis=0, concat_axis=1, tiled=True)  26 us
    all_to_all x1, blocking collectives, local(): lax.all_to_all(scores, 'expert', split_axis=0, concat_axis=1, tiled=True)  7.91 us
  transfers between devices with their start and end apart: 5, of which 4 were waited for; matrix products, arithmetic and copies ran while one was open for 2% of the time, Pallas kernels for 0%

commit v1 on v0

v1 whole, which is shorter than its diff:
```python
import functools

import jax
import jax.numpy as jnp
from jax import lax
from jax.experimental import pallas as pl
from jax.experimental.pallas import tpu as pltpu
from jax.sharding import Mesh, PartitionSpec as P

BF16 = jnp.bfloat16
F32 = jnp.float32
LANES = 128
PAD = 16
EXPERT = ("zl", "c")
VMEM = pl.BlockSpec(memory_space=pltpu.VMEM)
SMEM = pl.BlockSpec(memory_space=pltpu.SMEM)


def dot(a, b, ca, cb):
    return lax.dot_general(a, b, (((ca,), (cb,)), ((), ())), preferred_element_type=F32)


def call(kernel, out_shape, flops, *args, specs=None):
    nbytes = sum(a.size * a.dtype.itemsize for a in args)
    nbytes += out_shape.size * out_shape.dtype.itemsize
    return pl.pallas_call(
        kernel,
        out_shape=out_shape,
        in_specs=specs or [VMEM] * len(args),
        out_specs=VMEM,
        compiler_params=pltpu.CompilerParams(vmem_limit_bytes=40 << 20),
        cost_estimate=pl.CostEstimate(flops=flops, bytes_accessed=nbytes, transcendentals=0),
    )(*args)


def placed(picks_ref, e, tokens):
    row = picks_ref[pl.ds(e, 1), :]
    at = lax.broadcasted_iota(jnp.int32, (tokens, row.shape[1]), 0)
    return (at == row).astype(BF16)


def pick_kernel(y_ref, picks_ref, x_ref, g_ref, out_ref):
    experts, tokens = picks_ref.shape[0], x_ref.shape[0]
    share = out_ref.shape[2] // 2
    cols = pl.ds(pl.multiple_of(y_ref[0] * share, LANES), share)
    x, g = x_ref[:, cols], g_ref[:, cols]
    for e in range(experts):
        hot = placed(picks_ref, e, tokens)
        out_ref[e, :, :share] = dot(hot, x, 0, 0).astype(BF16)
        out_ref[e, :, share:] = dot(hot, g, 0, 0).astype(BF16)


def forward_kernel(xg_ref, gate_ref, up_ref, down_ref, out_ref):
    parts, _, both = xg_ref.shape
    share = both // 2
    hidden = gate_ref.shape[0]
    for i, (w_ref, at) in enumerate(((gate_ref, 0), (up_ref, 0), (down_ref, share))):
        total = None
        for k in range(parts):
            term = dot(xg_ref[k, :, at : at + share], w_ref[:, k * share : (k + 1) * share], 1, 1)
            total = term if total is None else total + term
        out_ref[:, i * hidden : (i + 1) * hidden] = total.astype(BF16)


def middle_kernel(part_ref, score_ref, out_ref):
    hidden = part_ref.shape[2] // 3

    def total(i):
        pieces = [part_ref[k, :, i * hidden : (i + 1) * hidden].astype(F32) for k in range(part_ref.shape[0])]
        return functools.reduce(lambda a, b: a + b, pieces)

    gate, up, back = total(0), total(1), total(2)
    sig = 1.0 / (1.0 + jnp.exp(-gate))
    act = gate * sig
    score = jnp.sum(act * up * back, axis=1, keepdims=True)
    grad_h = score_ref[...] * back
    out_ref[:, :hidden] = (grad_h * up * sig * (1.0 + gate * (1.0 - sig))).astype(BF16)
    out_ref[:, hidden : 2 * hidden] = (grad_h * act).astype(BF16)
    high = score.astype(BF16).astype(F32)
    lane = lax.broadcasted_iota(jnp.int32, (score.shape[0], LANES), 1)
    out_ref[:, 2 * hidden :] = jnp.where(lane == 0, high, jnp.where(lane == 1, score - high, 0.0)).astype(BF16)


def backward_kernel(d_ref, gate_ref, up_ref, out_ref):
    parts, _, share = out_ref.shape
    rows, hidden = d_ref.shape[0], gate_ref.shape[0]
    d_gate, d_up = d_ref[:, :hidden], d_ref[:, hidden : 2 * hidden]
    pick = (
        lax.broadcasted_iota(jnp.int32, (PAD, LANES), 0) == lax.broadcasted_iota(jnp.int32, (PAD, LANES), 1)
    ).astype(BF16)
    scores = dot(pick, d_ref[:, 2 * hidden :], 1, 1).astype(BF16)
    for k in range(parts):
        cols = slice(k * share, (k + 1) * share)
        total = dot(d_gate, gate_ref[:, cols], 1, 0) + dot(d_up, up_ref[:, cols], 1, 0)
        out_ref[k, :rows, :] = total.astype(BF16)
        out_ref[k, rows:, :] = scores


def scatter_kernel(picks_ref, rows_ref, out_ref):
    total = None
    for e in range(rows_ref.shape[0]):
        term = dot(placed(picks_ref, e, out_ref.shape[0]), rows_ref[e], 1, 0)
        total = term if total is None else total + term
    out_ref[...] = total.astype(BF16)


def exchange(a, axes):
    return lax.all_to_all(a, axes, split_axis=0, concat_axis=0, tiled=True)


def spread(a, axes, n):
    return exchange(jnp.broadcast_to(a[None], (n,) + a.shape), axes)


def local(sizes, layer_input, out_grad, scores, picks, w_gate, w_up, w_down):
    experts, taken = picks.shape
    tokens, width = layer_input.shape
    w_gate, w_up, w_down = w_gate[0], w_up[0], w_down[0]
    hidden = w_gate.shape[0]
    rows = experts * taken
    ny, nx, nh = sizes["y"], sizes["x"], sizes["zh"]
    share, block = width // ny, rows // nx

    y = lax.axis_index("y").astype(jnp.int32).reshape(1)
    sent = call(
        pick_kernel,
        jax.ShapeDtypeStruct((experts, taken, 2 * share), BF16),
        2 * rows * tokens * 2 * share,
        y, picks, layer_input, out_grad,
        specs=[SMEM, VMEM, VMEM, VMEM],
    )
    got = exchange(sent, EXPERT).reshape(rows, 2 * share)
    weight = exchange(scores.reshape(experts, 1, taken), EXPERT).reshape(rows)
    weight = lax.dynamic_slice(weight, (lax.axis_index("x") * block,), (block,))
    weight = weight.astype(F32).reshape(block, 1)
    xg = spread(got, "y", ny)
    part = call(
        forward_kernel,
        jax.ShapeDtypeStruct((rows, 3 * hidden), BF16),
        2 * rows * hidden * width * 3,
        xg, w_gate, w_up, w_down,
    )
    part = exchange(part.reshape(nx, block, 3 * hidden), "x")
    d_block = call(
        middle_kernel,
        jax.ShapeDtypeStruct((block, 2 * hidden + LANES), BF16),
        30 * block * hidden,
        part, weight,
    )
    d = spread(d_block, "x", nx).reshape(rows, 2 * hidden + LANES)
    part = call(
        backward_kernel,
        jax.ShapeDtypeStruct((ny, rows + PAD, share), BF16),
        4 * rows * hidden * width,
        d, w_gate, w_up,
    )
    part = exchange(part, "y")
    summed = jnp.sum(part.astype(F32), axis=0)
    row_part = summed[:rows].astype(BF16).reshape(experts, taken, share)
    score_part = (summed[rows] + summed[rows + 1]).reshape(experts, taken)
    high = score_part.astype(BF16)
    low = (score_part - high.astype(F32)).astype(BF16)
    score_part = jnp.stack([high, low], axis=1)
    score_all = exchange(
        jnp.broadcast_to(score_part[None], (nh,) + score_part.shape).reshape(nh * experts, 2, taken),
        ("zh",) + EXPERT,
    )
    score_grad = score_all.reshape(nh, experts, 2, taken).astype(F32).sum(axis=(0, 2)).astype(BF16)
    back = exchange(row_part, EXPERT)
    token_part = call(
        scatter_kernel,
        jax.ShapeDtypeStruct((tokens, share), BF16),
        2 * rows * tokens * share,
        picks, back,
    )
    token_grad = jnp.sum(spread(token_part, "zh", nh).astype(F32), axis=0).astype(BF16)
    input_grad = lax.all_gather(token_grad, "y", axis=1, tiled=True)
    return input_grad, score_grad


def solution(mesh):
    sizes = {"zl": 4, "c": 2, "y": 4, "zh": 4, "x": 4}
    fine = Mesh(mesh.devices.reshape(tuple(sizes.values())), tuple(sizes))
    ffn = ("y", "zh")
    placed_in = (
        P(EXPERT, "x"),
        P(EXPERT, "x"),
        P(None, EXPERT),
        P(None, EXPERT),
        P(EXPERT, ffn, "x"),
        P(EXPERT, ffn, "x"),
        P(EXPERT, ffn, "x"),
    )
    return jax.shard_map(
        functools.partial(local, sizes),
        mesh=fine,
        in_specs=placed_in,
        out_specs=(P(EXPERT, "x"), P(None, EXPERT)),
        check_vma=False,
    )
```

time: 377 us -> 207 us (0.55)
  the two profiles are of different devices: /device:TPU:2 before, /device:TPU:32 now
where the time goes in v1:
time: 207 us; the launch traced here: 206 us
  waiting for transfers between devices  86.7 us (42%)
  blocking collectives  67.5 us (33%)
  starting transfers between devices  33.5 us (16%)
  local copies, waits for them, and re-layouts  11.5 us (6%)
  Pallas kernels  5.06 us (2%)
    all_to_all x6, waiting for transfers between devices, exchange(): return lax.all_to_all(a, axes, split_axis=0, concat_axis=0, tiled=True)  86.7 us
    all_to_all x3, blocking collectives, exchange(): return lax.all_to_all(a, axes, split_axis=0, concat_axis=0, tiled=True)  54.8 us
    all_to_all x6, starting transfers between devices, exchange(): return lax.all_to_all(a, axes, split_axis=0, concat_axis=0, tiled=True)  33.5 us
    all_gather x1, blocking collectives, local(): input_grad = lax.all_gather(token_grad, 'y', axis=1, tiled=True)  12.7 us
    unnamed x21, local copies, waits for them, and re-layouts  6.89 us
    pallas_call x5, Pallas kernels, call(): pl.pallas_call(kernel, out_shape=out_shape, in_specs=specs or [VMEM] * le...  5.06 us
  transfers between devices with their start and end apart: 6, of which 5 were waited for; matrix products, arithmetic and copies ran while one was open for 1% of the time, Pallas kernels for 1%

profile of v1, /device:TPU:32, one launch (start us, length us, event | category | flops | bytes accessed | tf_op | source)
XLA Modules:
  0.0 206.0 jit_solution(7132878082053636782)
XLA Ops:
  0.6 1.0 copy-done.5
  1.6 1.0 copy-done.6
  2.6 0.7 copy-done.7
  3.3 0.5 shard_map.86
  3.8 23.0 %all_to_all.45 = bf16[8,48,768]{2,1,0:T(8,128)(2,1)S(1)} all-to-all(bf16[8,48,768]{2,1,0:T(8,128)(2,1)S(1)} %shard_map.86), channel_id=1, replica_groups=mesh['zl'=4,'c'=2,'y'=4,'zh'=4,'x'=4] {'zl','c'}, dimensions={0} | all-to-all | bytes 1179648 | tf_op jit(solution)/shard_map/all_to_all | solution.py:108
  26.8 1.6 broadcast_in_dim.11
  28.3 3.8 %all-to-all-start.1 = ((bf16[4,384,768]{2,1,0:T(8,128)(2,1)}), bf16[4,384,768]{2,1,0:T(8,128)(2,1)S(1)}, u32[]{:S(2)}, u32[]{:S(2)}) async-start(bf16[4,384,768]{2,1,0:T(8,128)(2,1)} %broadcast_in_dim.11), calls=%async_computation.1 | async-start | bytes 4718592 | tf_op jit(solution)/shard_map/all_to_all | solution.py:108
  32.1 0.6 copy.18
  32.7 28.7 %all-to-all-done.1.xg_ref = bf16[4,384,768]{2,1,0:T(8,128)(2,1)S(1)} async-done(((bf16[4,384,768]{2,1,0:T(8,128)(2,1)}), bf16[4,384,768]{2,1,0:T(8,128)(2,1)S(1)}, u32[]{:S(2)}, u32[]{:S(2)}) %all-to-all-start.1) | async-done | bytes 2359328 | tf_op jit(solution)/shard_map/all_to_all | solution.py:108
  61.4 4.9 %all-to-all-start.3 = ((bf16[8,1,48]{2,1,0:T(2,128)(2,1)}), bf16[8,1,48]{2,1,0:T(2,128)(2,1)S(1)}, u32[]{:S(2)}, u32[]{:S(2)}) async-start(bf16[8,1,48]{2,1,0:T(2,128)(2,1)} %copy.18), calls=%async_computation.3 | async-start | bytes 8192 | tf_op jit(solution)/shard_map/all_to_all | solution.py:108
  66.3 1.3 copy-done.1
  67.6 1.3 copy-done.4
  68.8 2.4 %shard_map.87 = bf16[384,1152]{1,0:T(8,128)(2,1)S(1)} custom-call(bf16[4,384,768]{2,1,0:T(8,128)(2,1)S(1)} %all-to-all-done.1.xg_ref, bf16[384,1536]{1,0:T(8,128)(2,1)S(1)} %bitcast.15, bf16[384,1536]{1,0:T(8,128)(2,1)S(1)} %bitcast.17, bf16[384,1536]{1,0:T(8,128)(2,1)S(1)} %bitcast.21), custom_call_target="tpu_custom_call" | custom-call | flops 1358954496 | bytes 6782976 | tf_op jit(solution)/shard_map/pallas_call | solution.py:26
  71.2 0.9 copy-done.3
  72.1 3.5 %all-to-all-start.2 = ((bf16[4,96,1152]{2,1,0:T(8,128)(2,1)}), bf16[4,96,1152]{2,1,0:T(8,128)(2,1)S(1)}, u32[]{:S(2)}, u32[]{:S(2)}) async-start(bf16[4,96,1152]{2,1,0:T(8,128)(2,1)} %bitcast.19), calls=%async_computation.2 | async-start | bytes 1769472 | tf_op jit(solution)/shard_map/all_to_all | solution.py:108
  75.9 13.6 %all-to-all-done.2.part_ref = bf16[4,96,1152]{2,1,0:T(8,128)(2,1)S(1)} async-done(((bf16[4,96,1152]{2,1,0:T(8,128)(2,1)}), bf16[4,96,1152]{2,1,0:T(8,128)(2,1)S(1)}, u32[]{:S(2)}, u32[]{:S(2)}) %all-to-all-start.2) | async-done | bytes 884768 | tf_op jit(solution)/shard_map/all_to_all | solution.py:108
  89.9 13.5 %all_to_all.46 = bf16[4,96,896]{2,1,0:T(8,128)(2,1)S(1)} all-to-all(bf16[4,96,896]{2,1,0:T(8,128)(2,1)S(1)} %broadcast_in_dim.12), channel_id=1, replica_groups=mesh['zl'=4,'c'=2,'y'=4,'zh'=4,'x'=4] {'x'}, dimensions={0} | all-to-all | bytes 1376256 | tf_op jit(solution)/shard_map/all_to_all | solution.py:108
  103.4 1.6 shard_map.89
  105.0 18.3 %all_to_all.47 = bf16[4,400,384]{2,1,0:T(8,128)(2,1)S(1)} all-to-all(bf16[4,400,384]{2,1,0:T(8,128)(2,1)S(1)} %shard_map.89), channel_id=1, replica_groups=mesh['zl'=4,'c'=2,'y'=4,'zh'=4,'x'=4] {'y'}, dimensions={0} | all-to-all | bytes 2457600 | tf_op jit(solution)/shard_map/all_to_all | solution.py:108
  123.5 0.7 slice.21
  124.2 5.1 %all-to-all-start.6 = ((bf16[8,48,384]{2,1,0:T(8,128)(2,1)}), bf16[8,48,384]{2,1,0:T(8,128)(2,1)S(1)}, u32[]{:S(2)}, u32[]{:S(2)}) async-start(bf16[8,48,384]{2,1,0:T(8,128)(2,1)} %bitcast.9), calls=%async_computation.6 | async-start | bytes 589824 | tf_op jit(solution)/shard_map/all_to_all | solution.py:108
  129.5 8.3 %all-to-all-done.6.rows_ref = bf16[8,48,384]{2,1,0:T(8,128)(2,1)S(1)} async-done(((bf16[8,48,384]{2,1,0:T(8,128)(2,1)}), bf16[8,48,384]{2,1,0:T(8,128)(2,1)S(1)}, u32[]{:S(2)}, u32[]{:S(2)}) %all-to-all-start.6) | async-done | bytes 294944 | tf_op jit(solution)/shard_map/all_to_all | solution.py:108
  137.8 0.6 broadcast_in_dim.14
  138.4 12.7 %all-to-all-start.8 = ((bf16[32,2,48]{2,1,0:T(2,128)(2,1)}), bf16[32,2,48]{2,1,0:T(2,128)(2,1)S(1)}, u32[]{:S(2)}, u32[]{:S(2)}) async-start(bf16[32,2,48]{2,1,0:T(2,128)(2,1)} %bitcast.10), calls=%async_computation.8 | async-start | bytes 32768 | tf_op jit(solution)/shard_map/all_to_all | solution.py:108
  151.1 0.3 shard_map.90
  151.5 10.8 %all-to-all-done.8 = bf16[32,2,48]{2,1,0:T(2,128)(2,1)S(1)} async-done(((bf16[32,2,48]{2,1,0:T(2,128)(2,1)}), bf16[32,2,48]{2,1,0:T(2,128)(2,1)S(1)}, u32[]{:S(2)}, u32[]{:S(2)}) %all-to-all-start.8) | async-done | bytes 6176 | tf_op jit(solution)/shard_map/all_to_all | solution.py:108
  162.3 0.8 broadcast_in_dim.13
  163.1 3.5 %all-to-all-start.7 = ((bf16[4,128,384]{2,1,0:T(8,128)(2,1)}), bf16[4,128,384]{2,1,0:T(8,128)(2,1)S(1)}, u32[]{:S(2)}, u32[]{:S(2)}) async-start(bf16[4,128,384]{2,1,0:T(8,128)(2,1)} %broadcast_in_dim.13), calls=%async_computation.7 | async-start | bytes 786432 | tf_op jit(solution)/shard_map/all_to_all | solution.py:108
  166.6 0.6 bitcast_reduce_fusion
  167.2 25.3 %all-to-all-done.7 = bf16[4,128,384]{2,1,0:T(8,128)(2,1)S(1)} async-done(((bf16[4,128,384]{2,1,0:T(8,128)(2,1)}), bf16[4,128,384]{2,1,0:T(8,128)(2,1)S(1)}, u32[]{:S(2)}, u32[]{:S(2)}) %all-to-all-start.7) | async-done | bytes 393248 | tf_op jit(solution)/shard_map/all_to_all | solution.py:108
  192.5 12.7 %all_gather.3 = bf16[128,1536]{1,0:T(8,128)(2,1)S(1)} all-gather(bf16[128,384]{1,0:T(8,128)(2,1)S(1)} %reduce_sum.41), channel_id=1, replica_groups=mesh['zl'=4,'c'=2,'y'=4,'zh'=4,'x'=4] {'y'}, dimensions={1}, use_global_device_ids=true | all-gather | bytes 491520 | tf_op jit(solution)/shard_map/all_gather | solution.py:177
  205.2 0.7 copy.24
  (29 shorter events, 1.1 us)
Async XLA Ops:
  0.6 1.0 copy-start.5
  1.6 1.0 copy-start.6
  2.6 0.7 copy-start.7
  28.3 3.8 %copy-start.9 = (bf16[8,48]{1,0:T(8,128)(2,1)S(1)}, bf16[8,48]{1,0:T(8,128)(2,1)}, u32[]{:S(2)}) copy-start(bf16[8,48]{1,0:T(8,128)(2,1)} %param.9) | copy-start | bytes 2308
  28.3 37.9 %copy-start = (bf16[1,384,1536]{2,1,0:T(8,128)(2,1)S(1)}, bf16[1,384,1536]{2,1,0:T(8,128)(2,1)}, u32[]{:S(2)}) copy-start(bf16[1,384,1536]{2,1,0:T(8,128)(2,1)} %param.11) | copy-start | bytes 3538948
  28.3 33.1 %all-to-all-start.1 = ((bf16[4,384,768]{2,1,0:T(8,128)(2,1)}), bf16[4,384,768]{2,1,0:T(8,128)(2,1)S(1)}, u32[]{:S(2)}, u32[]{:S(2)}) async-start(bf16[4,384,768]{2,1,0:T(8,128)(2,1)} %broadcast_in_dim.11), calls=%async_computation.1 | async-start | bytes 4718592 | tf_op jit(solution)/shard_map/all_to_all | solution.py:108
  61.4 10.7 %all-to-all-start.3 = ((bf16[8,1,48]{2,1,0:T(2,128)(2,1)}), bf16[8,1,48]{2,1,0:T(2,128)(2,1)S(1)}, u32[]{:S(2)}, u32[]{:S(2)}) async-start(bf16[8,1,48]{2,1,0:T(2,128)(2,1)} %copy.18), calls=%async_computation.3 | async-start | bytes 8192 | tf_op jit(solution)/shard_map/all_to_all | solution.py:108
  66.3 1.3 copy-start.1
  67.6 1.3 copy-start.4
  71.2 0.9 copy-start.3
  72.1 17.4 %all-to-all-start.2 = ((bf16[4,96,1152]{2,1,0:T(8,128)(2,1)}), bf16[4,96,1152]{2,1,0:T(8,128)(2,1)S(1)}, u32[]{:S(2)}, u32[]{:S(2)}) async-start(bf16[4,96,1152]{2,1,0:T(8,128)(2,1)} %bitcast.19), calls=%async_computation.2 | async-start | bytes 1769472 | tf_op jit(solution)/shard_map/all_to_all | solution.py:108
  89.8 13.6 %copy-start.2 = (bf16[1,384,1536]{2,1,0:T(8,128)(2,1)S(1)}, bf16[1,384,1536]{2,1,0:T(8,128)(2,1)}, u32[]{:S(2)}) copy-start(bf16[1,384,1536]{2,1,0:T(8,128)(2,1)} %param.12) | copy-start | bytes 3538948
  123.3 27.8 %copy-start.8 = (s32[8,48]{1,0:T(8,128)S(1)}, s32[8,48]{1,0:T(8,128)}, u32[]{:S(2)}) copy-start(s32[8,48]{1,0:T(8,128)} %picks_ref.3) | copy-start | bytes 4612
  124.2 13.5 %all-to-all-start.6 = ((bf16[8,48,384]{2,1,0:T(8,128)(2,1)}), bf16[8,48,384]{2,1,0:T(8,128)(2,1)S(1)}, u32[]{:S(2)}, u32[]{:S(2)}) async-start(bf16[8,48,384]{2,1,0:T(8,128)(2,1)} %bitcast.9), calls=%async_computation.6 | async-start | bytes 589824 | tf_op jit(solution)/shard_map/all_to_all | solution.py:108
  138.4 23.9 %all-to-all-start.8 = ((bf16[32,2,48]{2,1,0:T(2,128)(2,1)}), bf16[32,2,48]{2,1,0:T(2,128)(2,1)S(1)}, u32[]{:S(2)}, u32[]{:S(2)}) async-start(bf16[32,2,48]{2,1,0:T(2,128)(2,1)} %bitcast.10), calls=%async_computation.8 | async-start | bytes 32768 | tf_op jit(solution)/shard_map/all_to_all | solution.py:108
  163.1 29.4 %all-to-all-start.7 = ((bf16[4,128,384]{2,1,0:T(8,128)(2,1)}), bf16[4,128,384]{2,1,0:T(8,128)(2,1)S(1)}, u32[]{:S(2)}, u32[]{:S(2)}) async-start(bf16[4,128,384]{2,1,0:T(8,128)(2,1)} %broadcast_in_dim.13), calls=%async_computation.7 | async-start | bytes 786432 | tf_op jit(solution)/shard_map/all_to_all | solution.py:108

commit v2 on v1

v2 whole, which is shorter than its diff:
```python
import functools

import jax
import jax.numpy as jnp
from jax import lax
from jax.experimental import pallas as pl
from jax.experimental.pallas import tpu as pltpu
from jax.sharding import Mesh, PartitionSpec as P

BF16 = jnp.bfloat16
F32 = jnp.float32
LANES = 128
PAD = 16
EXPERT = ("zl", "c")
RING = ("zl", "c", "zh")
SIZES = {"zl": 4, "c": 2, "y": 4, "zh": 4, "x": 4}
LIMIT = 16
VMEM = pl.BlockSpec(memory_space=pltpu.VMEM)
SMEM = pl.BlockSpec(memory_space=pltpu.SMEM)


def dot(a, b, ca, cb):
    return lax.dot_general(a, b, (((ca,), (cb,)), ((), ())), preferred_element_type=F32)


def iota(shape, axis):
    return lax.broadcasted_iota(jnp.int32, shape, axis)


def sds(shape, dtype=BF16):
    return jax.ShapeDtypeStruct(shape, dtype)


def add_up(pieces):
    return functools.reduce(lambda a, b: a + b, pieces)


def call(kernel, outs, args, *, flops, specs=None, scratch=(), limit=LIMIT):
    nbytes = sum(a.size * a.dtype.itemsize for a in list(args) + jax.tree.leaves(outs))
    return pl.pallas_call(
        kernel,
        out_shape=outs,
        in_specs=specs or [VMEM] * len(args),
        out_specs=jax.tree.map(lambda o: VMEM, outs),
        scratch_shapes=scratch,
        compiler_params=pltpu.CompilerParams(vmem_limit_bytes=limit << 20),
        cost_estimate=pl.CostEstimate(flops=flops, bytes_accessed=nbytes, transcendentals=0),
    )(*args)


BLOCKS = ((0, 0), (0, 1), (1, 0), (-1, 0), (2, 0), (1, 1), (-1, 1), (2, 1))


def at(pos_ref, dz, dc):
    chips, cores = SIZES["zl"], SIZES["c"]
    return lax.rem(pos_ref[0] + (dz + chips), chips) * cores + lax.rem(pos_ref[1] + dc, cores)


def pick_kernel(pos_ref, picks_ref, xg_ref, own_ref, swap_ref, up_ref, down_ref, far_x_ref, far_g_ref, hot_ref):
    experts, taken = picks_ref.shape
    tokens, width = xg_ref.shape[1:]
    row = iota(picks_ref.shape, 0)
    taken_here = picks_ref[...].astype(F32)
    picked = [
        jnp.sum(jnp.where(row == at(pos_ref, *b), taken_here, 0.0), axis=0, keepdims=True) for b in BLOCKS
    ]
    picks = jnp.transpose(jnp.concatenate(picked, axis=0))
    lane = iota((taken, tokens), 1).astype(F32)
    for i in range(experts):
        hot_ref[i * taken : (i + 1) * taken, :] = (lane == picks[:, i : i + 1]).astype(BF16)
    step = 4 * LANES
    for which, far_ref in enumerate((far_x_ref, far_g_ref)):
        for start in range(0, width, step):
            cols = slice(start, start + step)
            rows = dot(hot_ref[...], xg_ref[which, :, cols], 1, 0).astype(BF16)
            blocks = [rows[i * taken : (i + 1) * taken] for i in range(experts)]
            own_ref[which, :, cols] = blocks[0]
            swap_ref[which, :, cols] = blocks[1]
            for dc in range(2):
                up_ref[dc, which, :, cols] = blocks[2 + 3 * dc]
                down_ref[dc, which, :, cols] = blocks[3 + 3 * dc]
                far_ref[dc, :, cols] = blocks[4 + 3 * dc]


def pass_kernel(up_ref, down_ref, far_x_ref, far_g_ref, out_ref):
    out_ref[0] = up_ref[1]
    out_ref[1] = down_ref[1]
    out_ref[2, 0] = far_x_ref[1]
    out_ref[2, 1] = far_g_ref[1]


def forward_kernel(*refs):
    own_ref, swap_ref, up_ref, down_ref, far_x_ref, far_g_ref, other_ref = refs[:7]
    gate_ref, up_w_ref, down_w_ref, out_ref, x_ref, g_ref = refs[7:]
    taken = own_ref.shape[1]
    for which, (far_ref, rows_ref) in enumerate(((far_x_ref, x_ref), (far_g_ref, g_ref))):
        blocks = [own_ref[which], swap_ref[which], up_ref[0, which], down_ref[0, which], far_ref[0]]
        blocks += [other_ref[i, which] for i in range(3)]
        for i, block in enumerate(blocks):
            rows_ref[i * taken : (i + 1) * taken, :] = block
    hidden = gate_ref.shape[0]
    for i, (w_ref, rows_ref) in enumerate(((gate_ref, x_ref), (up_w_ref, x_ref), (down_w_ref, g_ref))):
        total = dot(rows_ref[...], w_ref[...], 1, 1)
        out_ref[:, i * hidden : (i + 1) * hidden] = total.astype(BF16)


def middle_kernel(part_ref, out_ref):
    parts, block, _ = part_ref.shape
    hidden = part_ref.shape[2] // 3
    gate, up, back = (
        add_up([part_ref[k, :, i * hidden : (i + 1) * hidden].astype(F32) for k in range(parts)])
        for i in range(3)
    )
    sig = 1.0 / (1.0 + jnp.exp(-gate))
    act = gate * sig
    score = jnp.sum(act * up * back, axis=1, keepdims=True)
    out_ref[:, :hidden] = (back * up * sig * (1.0 + gate * (1.0 - sig))).astype(BF16)
    out_ref[:, hidden : 2 * hidden] = (back * act).astype(BF16)
    high = score.astype(BF16).astype(F32)
    lane = iota((block, LANES), 1)
    both = jnp.where(lane == 0, high, jnp.where(lane == 1, score - high, 0.0))
    out_ref[:, 2 * hidden :] = both.astype(BF16)


def score_block(d_scores, shards):
    rows = d_scores.shape[0]
    each = rows // shards
    pick = (iota((PAD, LANES), 0) == iota((PAD, LANES), 1)).astype(BF16)
    lines = dot(pick, d_scores, 1, 1)
    at = iota((PAD, rows), 0)
    shard = iota((PAD, rows), 1) // each
    apart = jnp.where(at == shard, lines[0:1, :], jnp.where(at == shard + shards, lines[1:2, :], 0.0))
    lane = iota((rows, LANES), 0) % each
    return dot(apart.astype(BF16), (iota((rows, LANES), 1) == lane).astype(BF16), 1, 0)


def backward_kernel(shards, d_ref, gate_ref, up_ref, out_ref):
    rows, hidden = d_ref.shape[0], gate_ref.shape[0]
    parts, _, share = out_ref.shape
    block = score_block(d_ref[:, 2 * hidden :], shards).astype(BF16)
    for k in range(parts):
        cols = slice(k * share, (k + 1) * share)
        total = dot(d_ref[:, :hidden], gate_ref[:, cols], 1, 0)
        total += dot(d_ref[:, hidden : 2 * hidden], up_ref[:, cols], 1, 0)
        out_ref[k, :rows, :] = total.astype(BF16)
        out_ref[k, rows:, :] = jnp.zeros((PAD, share), BF16)
        out_ref[k, rows:, :LANES] = block


def sum_kernel(pos_ref, part_ref, out_ref):
    parts, _, share = part_ref.shape
    shards, each, _ = out_ref.shape
    each -= PAD
    order = [at(pos_ref, -dz, dc) for dz, dc in BLOCKS]
    for j in range(shards):
        rows = slice(j * each, (j + 1) * each)
        total = add_up([part_ref[k, rows, :].astype(F32) for k in range(parts)])
        out_ref[order[j], :each, :] = total.astype(BF16)
    total = add_up([part_ref[k, shards * each :, :].astype(F32) for k in range(parts)])
    score = total[:shards] + total[shards:]
    high = score.astype(BF16).astype(F32)
    low = score - high
    row = iota((PAD, share), 0)
    for j in range(shards):
        both = jnp.where(row == 0, high[j : j + 1], jnp.where(row == 1, low[j : j + 1], 0.0))
        out_ref[order[j], each:, :] = both.astype(BF16)


def scatter_kernel(picks_ref, weights_ref, back_ref, out_ref):
    experts, taken = picks_ref.shape
    tokens, share = out_ref.shape[0] - PAD, out_ref.shape[1]
    weights = weights_ref[...].astype(F32)
    scores = jnp.zeros((PAD, share), F32)
    line = iota((PAD, share), 0)
    token = iota((tokens, taken), 0)
    terms = []
    for e in range(experts):
        lines = back_ref[e, taken:, :].astype(F32)
        scores = jnp.where(line == e, lines[0:1], jnp.where(line == e + experts, lines[1:2], scores))
        placed = jnp.where(token == picks_ref[e : e + 1, :], weights[e : e + 1, :], 0.0).astype(BF16)
        terms.append(dot(placed, back_ref[e, :taken, :], 1, 0))
    out_ref[:tokens, :] = add_up(terms).astype(BF16)
    out_ref[tokens:, :] = scores.astype(BF16)


def final_kernel(part_ref, grad_ref, score_ref):
    tokens = grad_ref.shape[0]
    experts, taken = score_ref.shape
    total = add_up([part_ref[k].astype(F32) for k in range(part_ref.shape[0])])
    grad_ref[...] = total[:tokens].astype(BF16)
    score = total[tokens : tokens + experts] + total[tokens + experts :]
    score_ref[...] = score[:, :taken].astype(BF16)


def exchange(a, axes):
    return lax.all_to_all(a, axes, split_axis=0, concat_axis=0, tiled=True)


def along_z(dz):
    nl, nc, nh = (SIZES[a] for a in RING)
    return [
        ((z % nl * nc + c) * nh + z // nl, (to % nl * nc + c) * nh + to // nl)
        for z in range(nl * nh)
        for to in [(z + dz) % (nl * nh)]
        for c in range(nc)
    ]


def local(layer_input, out_grad, scores, picks, w_gate, w_up, w_down):
    experts, taken = picks.shape
    tokens, width = layer_input.shape
    w_gate, w_up, w_down = w_gate[0], w_up[0], w_down[0]
    hidden = w_gate.shape[0]
    rows = experts * taken
    ny, nx = SIZES["y"], SIZES["x"]
    share, block = width // ny, rows // nx

    pos = jnp.stack([lax.axis_index(a).astype(jnp.int32) for a in EXPERT])
    one, two = sds((2, taken, width)), sds((2, 2, taken, width))
    own, swap, up, down, far_x, far_g = call(
        pick_kernel,
        [one, one, two, two, one, one],
        (pos, picks, jnp.stack([layer_input, out_grad])),
        flops=4 * rows * tokens * width,
        specs=[SMEM, VMEM, VMEM],
        scratch=[pltpu.VMEM((rows, tokens), BF16)],
    )
    up, down, far_x, far_g = (
        lax.ppermute(a, RING, along_z(dz)) for a, dz in ((up, 1), (down, -1), (far_x, 2), (far_g, -2))
    )

    across = [(0, 1), (1, 0)]
    swap = lax.ppermute(swap, "c", across)
    others = call(pass_kernel, sds((3, 2, taken, width)), (up, down, far_x, far_g), flops=0)
    others = lax.ppermute(others, "c", across)
    part = call(
        forward_kernel,
        sds((rows, 3 * hidden)),
        (own, swap, up, down, far_x, far_g, others, w_gate, w_up, w_down),
        flops=6 * rows * hidden * width,
        scratch=[pltpu.VMEM((rows, width), BF16)] * 2,
    )
    part = exchange(part.reshape(nx, block, 3 * hidden), "x")
    d_block = call(middle_kernel, sds((block, 2 * hidden + LANES)), (part,), flops=30 * block * hidden)
    d = lax.all_gather(d_block, "x", tiled=True)
    part = call(
        functools.partial(backward_kernel, experts),
        sds((ny, rows + PAD, share)),
        (d, w_gate, w_up),
        flops=4 * rows * hidden * width,
    )
    summed = call(
        sum_kernel,
        sds((experts, taken + PAD, share)),
        (pos, exchange(part, "y")),
        flops=4 * part.size,
        specs=[SMEM, VMEM],
    )
    back = exchange(summed, EXPERT)
    mine = call(
        scatter_kernel, sds((tokens + PAD, share)), (picks, scores, back), flops=2 * rows * tokens * share
    )
    token_grad, score_grad = call(
        final_kernel,
        [sds((tokens, share)), sds((experts, taken))],
        (lax.all_gather(mine, "zh"),),
        flops=4 * mine.size,
    )
    return lax.all_gather(token_grad, "y", axis=1, tiled=True), score_grad


def solution(mesh):
    fine = Mesh(mesh.devices.reshape(tuple(SIZES.values())), tuple(SIZES))
    ffn = ("y", "zh")
    placed_in = (
        P(EXPERT, "x"),
        P(EXPERT, "x"),
        P(None, EXPERT),
        P(None, EXPERT),
        P(EXPERT, ffn, "x"),
        P(EXPERT, ffn, "x"),
        P(EXPERT, ffn, "x"),
    )
    return jax.shard_map(
        local,
        mesh=fine,
        in_specs=placed_in,
        out_specs=(P(EXPERT, "x"), P(None, EXPERT)),
        check_vma=False,
    )
```

time: 207 us -> 158 us (0.76)
  the two profiles are of different devices: /device:TPU:32 before, /device:TPU:2 now
where the time goes in v2:
time: 158 us
  blocking collectives  104 us (66%)
  starting transfers between devices  25.7 us (16%)
  waiting for transfers between devices  18.3 us (12%)
  Pallas kernels  7.16 us (5%)
    all_to_all x3, blocking collectives, exchange(): return lax.all_to_all(a, axes, split_axis=0, concat_axis=0, tiled=True)  51.3 us
    all_gather x1, blocking collectives, local(): lax.all_gather(mine, 'zh')  26.9 us
    ppermute x4, starting transfers between devices, local(): lax.ppermute(a, RING, along_z(dz))  21.4 us
    ppermute x4, waiting for transfers between devices, local(): lax.ppermute(a, RING, along_z(dz))  17.1 us
    all_gather x1, blocking collectives, local(): d = lax.all_gather(d_block, 'x', tiled=True)  13 us
    all_gather x1, blocking collectives, local(): return (lax.all_gather(token_grad, 'y', axis=1, tiled=True), score_grad)  12.8 us
    pallas_call x8, Pallas kernels, call(): pl.pallas_call(kernel, out_shape=outs, in_specs=specs or [VMEM] * len(arg...  7.16 us
  transfers between devices with their start and end apart: 6, of which 3 were waited for; matrix products, arithmetic and copies ran while one was open for 0% of the time, Pallas kernels for 0%

profile of v2, /device:TPU:2, one launch (start us, length us, event | category | flops | bytes accessed | tf_op | source)
XLA Modules:
  0.0 158.1 jit_solution(12461215889729235774)
XLA Ops:
  0.6 0.1 pad_add_fusion.pos_ref
  0.7 1.2 pad_maximum_fusion.xg_ref
  1.9 0.0 copy-start.2
  1.9 1.5 shard_map.86
  3.4 3.8 %collective-permute-start.1 = (bf16[2,2,48,1536]{3,2,1,0:T(8,128)(2,1)S(1)}, bf16[2,2,48,1536]{3,2,1,0:T(8,128)(2,1)S(1)}, u32[]{:S(2)}, u32[]{:S(2)}) collective-permute-start(bf16[2,2,48,1536]{3,2,1,0:T(8,128)(2,1)S(1)} %get-tuple-element.12), channel_id=1, source_target_pairs={{0,128},{64,192},{128,256},{192,320},{256,384},{320,448},{384,4},{... | collective-permute-start | bytes 1769480 | tf_op jit(solution)/shard_map/ppermute | solution.py:229
  7.3 9.5 %collective-permute-start.2 = (bf16[2,2,48,1536]{3,2,1,0:T(8,128)(2,1)S(1)}, bf16[2,2,48,1536]{3,2,1,0:T(8,128)(2,1)S(1)}, u32[]{:S(2)}, u32[]{:S(2)}) collective-permute-start(bf16[2,2,48,1536]{3,2,1,0:T(8,128)(2,1)S(1)} %get-tuple-element.13), channel_id=1, source_target_pairs={{0,396},{64,460},{128,0},{192,64},{256,128},{320,192},{384,256},{4... | collective-permute-start | bytes 1769480 | tf_op jit(solution)/shard_map/ppermute | solution.py:229
  16.8 1.9 %collective-permute-start.3 = (bf16[2,48,1536]{2,1,0:T(8,128)(2,1)S(1)}, bf16[2,48,1536]{2,1,0:T(8,128)(2,1)S(1)}, u32[]{:S(2)}, u32[]{:S(2)}) collective-permute-start(bf16[2,48,1536]{2,1,0:T(8,128)(2,1)S(1)} %get-tuple-element.14), channel_id=1, source_target_pairs={{0,256},{64,320},{128,384},{192,448},{256,4},{320,68},{384,132},{4... | collective-permute-start | bytes 884744 | tf_op jit(solution)/shard_map/ppermute | solution.py:229
  18.7 0.0 copy-start
  18.7 0.0 copy-start.1
  18.7 6.2 %collective-permute-start.4 = (bf16[2,48,1536]{2,1,0:T(8,128)(2,1)S(1)}, bf16[2,48,1536]{2,1,0:T(8,128)(2,1)S(1)}, u32[]{:S(2)}, u32[]{:S(2)}) collective-permute-start(bf16[2,48,1536]{2,1,0:T(8,128)(2,1)S(1)} %get-tuple-element.15), channel_id=1, source_target_pairs={{0,268},{64,332},{128,396},{192,460},{256,0},{320,64},{384,128},{4... | collective-permute-start | bytes 884744 | tf_op jit(solution)/shard_map/ppermute | solution.py:229
  24.9 12.5 %collective-permute-done.3.far_x_ref.refs_4_ = bf16[2,48,1536]{2,1,0:T(8,128)(2,1)S(1)} collective-permute-done((bf16[2,48,1536]{2,1,0:T(8,128)(2,1)S(1)}, bf16[2,48,1536]{2,1,0:T(8,128)(2,1)S(1)}, u32[]{:S(2)}, u32[]{:S(2)}) %collective-permute-start.3) | collective-permute-done | bytes 294944 | tf_op jit(solution)/shard_map/ppermute | solution.py:229
  37.4 4.6 %collective-permute-done.4.far_g_ref.refs_5_ = bf16[2,48,1536]{2,1,0:T(8,128)(2,1)S(1)} collective-permute-done((bf16[2,48,1536]{2,1,0:T(8,128)(2,1)S(1)}, bf16[2,48,1536]{2,1,0:T(8,128)(2,1)S(1)}, u32[]{:S(2)}, u32[]{:S(2)}) %collective-permute-start.4) | collective-permute-done | bytes 294944 | tf_op jit(solution)/shard_map/ppermute | solution.py:229
  42.0 0.0 collective-permute-done.1.up_ref.refs_2_
  42.0 0.0 collective-permute-done.2.down_ref.refs_3_
  42.0 0.1 shard_map.87
  42.0 1.9 %collective-permute-start.5 = (bf16[3,2,48,1536]{3,2,1,0:T(8,128)(2,1)S(1)}, bf16[3,2,48,1536]{3,2,1,0:T(8,128)(2,1)S(1)}, u32[]{:S(2)}, u32[]{:S(2)}) collective-permute-start(bf16[3,2,48,1536]{3,2,1,0:T(8,128)(2,1)S(1)} %shard_map.87), channel_id=1, source_target_pairs={{0,64},{64,0},{1,65},{65,1},{2,66},{66,2},{3,67},{67,3},{4,68},{68... | collective-permute-start | bytes 2654216 | tf_op jit(solution)/shard_map/ppermute | solution.py:235
  44.0 2.4 %collective-permute-start = (bf16[2,48,1536]{2,1,0:T(8,128)(2,1)S(1)}, bf16[2,48,1536]{2,1,0:T(8,128)(2,1)S(1)}, u32[]{:S(2)}, u32[]{:S(2)}) collective-permute-start(bf16[2,48,1536]{2,1,0:T(8,128)(2,1)S(1)} %get-tuple-element.11), channel_id=1, source_target_pairs={{0,64},{64,0},{1,65},{65,1},{2,66},{66,2},{3,67},{67,3},{4,68},{68... | collective-permute-start | bytes 884744 | tf_op jit(solution)/shard_map/ppermute | solution.py:233
  46.4 1.2 collective-permute-done.refs_1_
  47.6 0.0 collective-permute-done.5.refs_6_
  47.6 2.0 %shard_map.88 = bf16[384,1152]{1,0:T(8,128)(2,1)S(1)} custom-call(bf16[2,48,1536]{2,1,0:T(8,128)(2,1)S(1)} %get-tuple-element.10.refs_0_, bf16[2,48,1536]{2,1,0:T(8,128)(2,1)S(1)} %collective-permute-done.refs_1_, bf16[2,2,48,1536]{3,2,1,0:T(8,128)(2,1)S(1)} %collective-permute-done.1.up_ref.refs_2_, ...), custom_call_target="tpu_custom_call" | custom-call | flops 1358954496 | bytes 7667712 | tf_op jit(solution)/shard_map/pallas_call | solution.py:40
  49.6 17.0 %all_to_all.15.part_ref = bf16[4,96,1152]{2,1,0:T(8,128)(2,1)S(1)} all-to-all(bf16[4,96,1152]{2,1,0:T(8,128)(2,1)S(1)} %bitcast.13), channel_id=1, replica_groups=mesh['zl'=4,'c'=2,'y'=4,'zh'=4,'x'=4] {'x'}, dimensions={0} | all-to-all | bytes 1769472 | tf_op jit(solution)/shard_map/all_to_all | solution.py:196
  66.6 0.2 shard_map.89
  66.9 13.0 %all_gather.12.d_ref = bf16[384,896]{1,0:T(8,128)(2,1)S(1)} all-gather(bf16[96,896]{1,0:T(8,128)(2,1)S(1)} %shard_map.89), channel_id=1, replica_groups=mesh['zl'=4,'c'=2,'y'=4,'zh'=4,'x'=4] {'x'}, dimensions={0}, use_global_device_ids=true | all-gather | bytes 860160 | tf_op jit(solution)/shard_map/all_gather | solution.py:245
  79.9 1.7 %shard_map.90 = bf16[4,400,384]{2,1,0:T(8,128)(2,1)S(1)} custom-call(bf16[384,896]{1,0:T(8,128)(2,1)S(1)} %all_gather.12.d_ref, bf16[384,1536]{1,0:T(8,128)(2,1)S(1)} %bitcast.10, bf16[384,1536]{1,0:T(8,128)(2,1)S(1)} %bitcast.12), custom_call_target="tpu_custom_call" | custom-call | flops 905969664 | bytes 4276224 | tf_op jit(solution)/shard_map/pallas_call | solution.py:40
  81.7 18.7 %all_to_all.16.part_ref = bf16[4,400,384]{2,1,0:T(8,128)(2,1)S(1)} all-to-all(bf16[4,400,384]{2,1,0:T(8,128)(2,1)S(1)} %shard_map.90), channel_id=1, replica_groups=mesh['zl'=4,'c'=2,'y'=4,'zh'=4,'x'=4] {'y'}, dimensions={0} | all-to-all | bytes 2457600 | tf_op jit(solution)/shard_map/all_to_all | solution.py:196
  100.3 0.7 shard_map.91
  101.0 15.6 %all_to_all.17.back_ref = bf16[8,64,384]{2,1,0:T(8,128)(2,1)S(1)} all-to-all(bf16[8,64,384]{2,1,0:T(8,128)(2,1)S(1)} %shard_map.91), channel_id=1, replica_groups=mesh['zl'=4,'c'=2,'y'=4,'zh'=4,'x'=4] {'zl','c'}, dimensions={0} | all-to-all | bytes 786432 | tf_op jit(solution)/shard_map/all_to_all | solution.py:196
  116.7 0.3 shard_map.92
  117.0 26.9 %all-gather = bf16[576,384]{1,0:T(8,128)(2,1)S(1)} all-gather(bf16[144,384]{1,0:T(8,128)(2,1)S(1)} %shard_map.92), channel_id=2, replica_groups=mesh['zl'=4,'c'=2,'y'=4,'zh'=4,'x'=4] {'zh'}, dimensions={0}, use_global_device_ids=true | all-gather | bytes 552960 | tf_op jit(solution)/shard_map/all_gather | solution.py:266
  143.9 0.6 shard_map.93
  144.5 12.8 %all_gather.15 = bf16[128,1536]{1,0:T(8,128)(2,1)S(1)} all-gather(bf16[128,384]{1,0:T(8,128)(2,1)S(1)} %get-tuple-element.16), channel_id=1, replica_groups=mesh['zl'=4,'c'=2,'y'=4,'zh'=4,'x'=4] {'y'}, dimensions={1}, use_global_device_ids=true | all-gather | bytes 491520 | tf_op jit(solution)/shard_map/all_gather | solution.py:269
  157.3 0.7 copy.10
  (7 shorter events, 0.0 us)
Async XLA Ops:
  0.6 1.3 copy-start.3
  1.9 45.6 %copy-start.2 = (bf16[1,384,1536]{2,1,0:T(8,128)(2,1)S(1)}, bf16[1,384,1536]{2,1,0:T(8,128)(2,1)}, u32[]{:S(2)}) copy-start(bf16[1,384,1536]{2,1,0:T(8,128)(2,1)} %param.13) | copy-start | bytes 3538948
  3.4 38.5 %collective-permute-start.1 = (bf16[2,2,48,1536]{3,2,1,0:T(8,128)(2,1)S(1)}, bf16[2,2,48,1536]{3,2,1,0:T(8,128)(2,1)S(1)}, u32[]{:S(2)}, u32[]{:S(2)}) collective-permute-start(bf16[2,2,48,1536]{3,2,1,0:T(8,128)(2,1)S(1)} %get-tuple-element.12), channel_id=1, source_target_pairs={{0,128},{64,192},{128,256},{192,320},{256,384},{320,448},{384,4},{... | collective-permute-start | bytes 1769480 | tf_op jit(solution)/shard_map/ppermute | solution.py:229
  7.3 34.7 %collective-permute-start.2 = (bf16[2,2,48,1536]{3,2,1,0:T(8,128)(2,1)S(1)}, bf16[2,2,48,1536]{3,2,1,0:T(8,128)(2,1)S(1)}, u32[]{:S(2)}, u32[]{:S(2)}) collective-permute-start(bf16[2,2,48,1536]{3,2,1,0:T(8,128)(2,1)S(1)} %get-tuple-element.13), channel_id=1, source_target_pairs={{0,396},{64,460},{128,0},{192,64},{256,128},{320,192},{384,256},{4... | collective-permute-start | bytes 1769480 | tf_op jit(solution)/shard_map/ppermute | solution.py:229
  16.8 20.6 %collective-permute-start.3 = (bf16[2,48,1536]{2,1,0:T(8,128)(2,1)S(1)}, bf16[2,48,1536]{2,1,0:T(8,128)(2,1)S(1)}, u32[]{:S(2)}, u32[]{:S(2)}) collective-permute-start(bf16[2,48,1536]{2,1,0:T(8,128)(2,1)S(1)} %get-tuple-element.14), channel_id=1, source_target_pairs={{0,256},{64,320},{128,384},{192,448},{256,4},{320,68},{384,132},{4... | collective-permute-start | bytes 884744 | tf_op jit(solution)/shard_map/ppermute | solution.py:229
  18.7 28.9 %copy-start = (bf16[1,384,1536]{2,1,0:T(8,128)(2,1)S(1)}, bf16[1,384,1536]{2,1,0:T(8,128)(2,1)}, u32[]{:S(2)}) copy-start(bf16[1,384,1536]{2,1,0:T(8,128)(2,1)} %param.11) | copy-start | bytes 3538948
  18.7 28.9 %copy-start.1 = (bf16[1,384,1536]{2,1,0:T(8,128)(2,1)S(1)}, bf16[1,384,1536]{2,1,0:T(8,128)(2,1)}, u32[]{:S(2)}) copy-start(bf16[1,384,1536]{2,1,0:T(8,128)(2,1)} %param.12) | copy-start | bytes 3538948
  18.7 23.3 %collective-permute-start.4 = (bf16[2,48,1536]{2,1,0:T(8,128)(2,1)S(1)}, bf16[2,48,1536]{2,1,0:T(8,128)(2,1)S(1)}, u32[]{:S(2)}, u32[]{:S(2)}) collective-permute-start(bf16[2,48,1536]{2,1,0:T(8,128)(2,1)S(1)} %get-tuple-element.15), channel_id=1, source_target_pairs={{0,268},{64,332},{128,396},{192,460},{256,0},{320,64},{384,128},{4... | collective-permute-start | bytes 884744 | tf_op jit(solution)/shard_map/ppermute | solution.py:229
  42.0 5.5 %collective-permute-start.5 = (bf16[3,2,48,1536]{3,2,1,0:T(8,128)(2,1)S(1)}, bf16[3,2,48,1536]{3,2,1,0:T(8,128)(2,1)S(1)}, u32[]{:S(2)}, u32[]{:S(2)}) collective-permute-start(bf16[3,2,48,1536]{3,2,1,0:T(8,128)(2,1)S(1)} %shard_map.87), channel_id=1, source_target_pairs={{0,64},{64,0},{1,65},{65,1},{2,66},{66,2},{3,67},{67,3},{4,68},{68... | collective-permute-start | bytes 2654216 | tf_op jit(solution)/shard_map/ppermute | solution.py:235
  44.0 3.6 %collective-permute-start = (bf16[2,48,1536]{2,1,0:T(8,128)(2,1)S(1)}, bf16[2,48,1536]{2,1,0:T(8,128)(2,1)S(1)}, u32[]{:S(2)}, u32[]{:S(2)}) collective-permute-start(bf16[2,48,1536]{2,1,0:T(8,128)(2,1)S(1)} %get-tuple-element.11), channel_id=1, source_target_pairs={{0,64},{64,0},{1,65},{65,1},{2,66},{66,2},{3,67},{67,3},{4,68},{68... | collective-permute-start | bytes 884744 | tf_op jit(solution)/shard_map/ppermute | solution.py:233
  100.3 16.4 %copy-start.4 = (bf16[8,48]{1,0:T(8,128)(2,1)S(1)}, bf16[8,48]{1,0:T(8,128)(2,1)}, u32[]{:S(2)}) copy-start(bf16[8,48]{1,0:T(8,128)(2,1)} %weights_ref.1) | copy-start | bytes 2308

commit v3 on v2

v3 whole, which is shorter than its diff:
```python
import functools

import jax
import jax.numpy as jnp
from jax import lax
from jax.experimental import pallas as pl
from jax.experimental.pallas import tpu as pltpu
from jax.sharding import Mesh, PartitionSpec as P

BF16 = jnp.bfloat16
F32 = jnp.float32
LANES = 128
PAD = 16
TAIL = 8
EXPERT = ("zl", "c")
RING = ("zl", "c", "zh")
SIZES = {"zl": 4, "c": 2, "y": 4, "zh": 4, "x": 4}
LIMIT = 16
VMEM = pl.BlockSpec(memory_space=pltpu.VMEM)
SMEM = pl.BlockSpec(memory_space=pltpu.SMEM)


def dot(a, b, ca, cb):
    return lax.dot_general(a, b, (((ca,), (cb,)), ((), ())), preferred_element_type=F32)


def iota(shape, axis):
    return lax.broadcasted_iota(jnp.int32, shape, axis)


def sds(shape, dtype=BF16):
    return jax.ShapeDtypeStruct(shape, dtype)


def add_up(pieces):
    return functools.reduce(lambda a, b: a + b, pieces)


def call(kernel, outs, args, *, flops, specs=None, scratch=(), limit=LIMIT):
    nbytes = sum(a.size * a.dtype.itemsize for a in list(args) + jax.tree.leaves(outs))
    return pl.pallas_call(
        kernel,
        out_shape=outs,
        in_specs=specs or [VMEM] * len(args),
        out_specs=jax.tree.map(lambda o: VMEM, outs),
        scratch_shapes=scratch,
        compiler_params=pltpu.CompilerParams(vmem_limit_bytes=limit << 20),
        cost_estimate=pl.CostEstimate(flops=flops, bytes_accessed=nbytes, transcendentals=0),
    )(*args)


BLOCKS = ((0, 0), (0, 1), (1, 0), (-1, 0), (1, 1), (-1, 1), (2, 0), (-2, 1))
NEAR = 6
NEAR_COST, FAR_COST = 1, 10
SENT = (2, 3, 4, 5, 1, 6, 7)


def at(pos_ref, dz, dc):
    chips, cores = SIZES["zl"], SIZES["c"]
    return lax.rem(pos_ref[0] + (dz + chips), chips) * cores + lax.rem(pos_ref[1] + dc, cores)


def pick_kernel(pos_ref, picks_ref, xg_ref, *refs):
    *outs, hot_ref = refs
    experts, taken = picks_ref.shape
    tokens, width = xg_ref.shape[1:]
    row = iota(picks_ref.shape, 0)
    values = picks_ref[...].astype(F32)
    picked = [
        jnp.sum(jnp.where(row == at(pos_ref, *b), values, 0.0), axis=0, keepdims=True) for b in BLOCKS
    ]
    picks = jnp.transpose(jnp.concatenate(picked, axis=0))
    lane = iota((taken, tokens), 1).astype(F32)
    for i in range(experts):
        hot_ref[i * taken : (i + 1) * taken, :] = (lane == picks[:, i : i + 1]).astype(BF16)
    step = 4 * LANES
    for which in range(2):
        for start in range(0, width, step):
            cols = slice(start, start + step)
            rows = dot(hot_ref[...], xg_ref[which, :, cols], 1, 0).astype(BF16)
            for i in range(experts):
                outs[i][which, :, cols] = rows[i * taken : (i + 1) * taken]


def after_kernel(a_ref, _, out_ref):
    out_ref[...] = a_ref[...]


def forward_kernel(*refs):
    blocks, (gate_ref, up_ref, down_ref, out_ref, x_ref, g_ref) = refs[:-6], refs[-6:]
    taken = blocks[0].shape[1]
    for which, rows_ref in enumerate((x_ref, g_ref)):
        for i, block in enumerate(blocks):
            rows_ref[i * taken : (i + 1) * taken, :] = block[which]
    hidden = gate_ref.shape[0]
    for i, (w_ref, rows_ref) in enumerate(((gate_ref, x_ref), (up_ref, x_ref), (down_ref, g_ref))):
        total = dot(rows_ref[...], w_ref[...], 1, 1)
        out_ref[:, i * hidden : (i + 1) * hidden] = total.astype(BF16)


def middle_kernel(*refs):
    *part_refs, out_ref = refs
    hidden = part_refs[0].shape[2] // 3

    def total(i):
        cols = slice(i * hidden, (i + 1) * hidden)
        sums = [add_up([ref[k, :, cols].astype(F32) for k in range(ref.shape[0])]) for ref in part_refs]
        return jnp.concatenate(sums, axis=0)

    gate, up, back = total(0), total(1), total(2)
    sig = 1.0 / (1.0 + jnp.exp(-gate))
    act = gate * sig
    score = jnp.sum(act * up * back, axis=1, keepdims=True)
    out_ref[:, :hidden] = (back * up * sig * (1.0 + gate * (1.0 - sig))).astype(BF16)
    out_ref[:, hidden : 2 * hidden] = (back * act).astype(BF16)
    high = score.astype(BF16).astype(F32)
    lane = iota((out_ref.shape[0], LANES), 1)
    both = jnp.where(lane == 0, high, jnp.where(lane == 1, score - high, 0.0))
    out_ref[:, 2 * hidden :] = both.astype(BF16)


def in_blocks(row, rows):
    parts = SIZES["x"]
    near = rows * NEAR // len(BLOCKS)
    x, r = row // (rows // parts), row % (rows // parts)
    near_x = near // parts
    return jnp.where(r < near_x, x * near_x + r, near + x * (rows // parts - near_x) + r - near_x)


def score_block(d_scores, shards):
    rows = d_scores.shape[0]
    each = rows // shards
    pick = (iota((PAD, LANES), 0) == iota((PAD, LANES), 1)).astype(BF16)
    lines = dot(pick, d_scores, 1, 1)
    line = iota((PAD, rows), 0)
    block = in_blocks(iota((PAD, rows), 1), rows) // each
    apart = jnp.where(line == block, lines[0:1, :], jnp.where(line == block + shards, lines[1:2, :], 0.0))
    lane = in_blocks(iota((rows, LANES), 0), rows) % each
    return dot(apart.astype(BF16), (iota((rows, LANES), 1) == lane).astype(BF16), 1, 0)


def backward_kernel(shards, d_ref, gate_ref, up_ref, out_ref):
    rows, hidden = d_ref.shape[0], gate_ref.shape[0]
    parts, _, share = out_ref.shape
    block = score_block(d_ref[:, 2 * hidden :], shards).astype(BF16)
    for k in range(parts):
        cols = slice(k * share, (k + 1) * share)
        total = dot(d_ref[:, :hidden], gate_ref[:, cols], 1, 0)
        total += dot(d_ref[:, hidden : 2 * hidden], up_ref[:, cols], 1, 0)
        out_ref[k, :rows, :] = total.astype(BF16)
        out_ref[k, rows:, :] = jnp.zeros((PAD, share), BF16)
        out_ref[k, rows:, :LANES] = block


def sum_kernel(pos_ref, part_ref, out_ref):
    parts, _, share = part_ref.shape
    shards, each, _ = out_ref.shape
    each -= TAIL
    rows = shards * each
    total = add_up([part_ref[k].astype(F32) for k in range(parts)])
    one = rows // SIZES["x"]
    near = one * NEAR // len(BLOCKS)
    ordered = [total[x * one : x * one + near] for x in range(SIZES["x"])]
    ordered += [total[x * one + near : (x + 1) * one] for x in range(SIZES["x"])]
    ordered = jnp.concatenate(ordered, axis=0)
    score = total[rows : rows + shards] + total[rows + shards :]
    high = score.astype(BF16).astype(F32)
    low = score - high
    row = iota((TAIL, share), 0)
    for i, (dz, dc) in enumerate(BLOCKS):
        both = jnp.where(row == 0, high[i : i + 1], jnp.where(row == 1, low[i : i + 1], 0.0))
        block = jnp.concatenate([ordered[i * each : (i + 1) * each], both], axis=0)
        out_ref[at(pos_ref, -dz, dc)] = block.astype(BF16)


def scatter_kernel(picks_ref, weights_ref, back_ref, out_ref):
    experts, taken = picks_ref.shape
    tokens, share = out_ref.shape[0] - PAD, out_ref.shape[1]
    weights = weights_ref[...].astype(F32)
    scores = jnp.zeros((PAD, share), F32)
    line = iota((PAD, share), 0)
    token = iota((tokens, taken), 0)
    terms = []
    for e in range(experts):
        block = back_ref[e].astype(F32)
        lines = block[taken:]
        scores = jnp.where(line == e, lines[0:1], jnp.where(line == e + experts, lines[1:2], scores))
        placed = jnp.where(token == picks_ref[e : e + 1, :], weights[e : e + 1, :], 0.0).astype(BF16)
        terms.append(dot(placed, block[:taken].astype(BF16), 1, 0))
    out_ref[:tokens, :] = add_up(terms).astype(BF16)
    out_ref[tokens:, :] = scores.astype(BF16)


def final_kernel(part_ref, grad_ref, score_ref):
    tokens = grad_ref.shape[0]
    experts, taken = score_ref.shape
    total = add_up([part_ref[k].astype(F32) for k in range(part_ref.shape[0])])
    grad_ref[...] = total[:tokens].astype(BF16)
    score = total[tokens : tokens + experts] + total[tokens + experts :]
    score_ref[...] = score[:, :taken].astype(BF16)


def exchange(a, axes):
    return lax.all_to_all(a, axes, split_axis=0, concat_axis=0, tiled=True)


def along_z(dz, dc):
    nl, nc, nh = (SIZES[a] for a in RING)
    return [
        ((z % nl * nc + c) * nh + z // nl, (to % nl * nc + (c + dc) % nc) * nh + to // nl)
        for z in range(nl * nh)
        for to in [(z + dz) % (nl * nh)]
        for c in range(nc)
    ]


def local(layer_input, out_grad, scores, picks, w_gate, w_up, w_down):
    experts, taken = picks.shape
    tokens, width = layer_input.shape
    w_gate, w_up, w_down = w_gate[0], w_up[0], w_down[0]
    hidden = w_gate.shape[0]
    rows = experts * taken
    ny, nx = SIZES["y"], SIZES["x"]
    share, block = width // ny, rows // nx

    pos = jnp.stack([lax.axis_index(a).astype(jnp.int32) for a in EXPERT])
    sent = call(
        pick_kernel,
        [sds((2, taken, width))] * experts,
        (pos, picks, jnp.stack([layer_input, out_grad])),
        flops=4 * rows * tokens * width,
        specs=[SMEM, VMEM, VMEM],
        scratch=[pltpu.VMEM((rows, tokens), BF16)],
    )
    got = {0: sent[0]}
    for i in SENT:
        got[i] = lax.ppermute(sent[i], RING, along_z(*BLOCKS[i]))

    def project(blocks, factor):
        count = len(blocks) * taken
        return call(
            forward_kernel,
            sds((count, 3 * hidden)),
            (*blocks, w_gate, w_up, w_down),
            flops=int(factor * 6 * count * hidden * width),
            scratch=[pltpu.VMEM((count, width), BF16)] * 2,
        )

    def over_x(a):
        return exchange(a.reshape(nx, a.shape[0] // nx, 3 * hidden), "x")

    near = over_x(project([got[i] for i in range(NEAR)], NEAR_COST))
    far = project([got[i] for i in range(NEAR, experts)], FAR_COST)
    far = over_x(call(after_kernel, sds(far.shape), (far, near), flops=0))
    parts = (near, far)
    d_block = call(middle_kernel, sds((block, 2 * hidden + LANES)), parts, flops=30 * block * hidden)
    d = lax.all_gather(d_block, "x", tiled=True)
    part = call(
        functools.partial(backward_kernel, experts),
        sds((ny, rows + PAD, share)),
        (d, w_gate, w_up),
        flops=4 * rows * hidden * width,
    )
    summed = call(
        sum_kernel,
        sds((experts, taken + TAIL, share)),
        (pos, exchange(part, "y")),
        flops=4 * part.size,
        specs=[SMEM, VMEM],
    )
    back = exchange(summed, EXPERT)
    mine = call(
        scatter_kernel, sds((tokens + PAD, share)), (picks, scores, back), flops=2 * rows * tokens * share
    )
    token_grad, score_grad = call(
        final_kernel,
        [sds((tokens, share)), sds((experts, taken))],
        (lax.all_gather(mine, "zh"),),
        flops=4 * mine.size,
    )
    return lax.all_gather(token_grad, "y", axis=1, tiled=True), score_grad


def solution(mesh):
    fine = Mesh(mesh.devices.reshape(tuple(SIZES.values())), tuple(SIZES))
    ffn = ("y", "zh")
    placed_in = (
        P(EXPERT, "x"),
        P(EXPERT, "x"),
        P(None, EXPERT),
        P(None, EXPERT),
        P(EXPERT, ffn, "x"),
        P(EXPERT, ffn, "x"),
        P(EXPERT, ffn, "x"),
    )
    return jax.shard_map(
        local,
        mesh=fine,
        in_specs=placed_in,
        out_specs=(P(EXPERT, "x"), P(None, EXPERT)),
        check_vma=False,
    )
```

time: 158 us -> 152 us (0.962)
  the two profiles are of different devices: /device:TPU:2 before, /device:TPU:4 now
where the time goes in v3:
time: 152 us; the launch traced here: 151 us
  blocking collectives  95.5 us (63%)
  starting transfers between devices  34.3 us (23%)
  Pallas kernels  9.65 us (6%)
  waiting for transfers between devices  5.29 us (3%)
  local copies, waits for them, and re-layouts  4.13 us (3%)
    all_to_all x3, blocking collectives, exchange(): return lax.all_to_all(a, axes, split_axis=0, concat_axis=0, tiled=True)  41.3 us
    ppermute x7, starting transfers between devices, local(): got[i] = lax.ppermute(sent[i], RING, along_z(*BLOCKS[i]))  29.5 us
    all_gather x1, blocking collectives, local(): lax.all_gather(mine, 'zh')  26.9 us
    all_gather x1, blocking collectives, local(): d = lax.all_gather(d_block, 'x', tiled=True)  14 us
    all_gather x1, blocking collectives, local(): return (lax.all_gather(token_grad, 'y', axis=1, tiled=True), score_grad)  13.3 us
    pallas_call x9, Pallas kernels, call(): pl.pallas_call(kernel, out_shape=outs, in_specs=specs or [VMEM] * len(arg...  9.65 us
    all_to_all x1, starting transfers between devices, exchange(): return lax.all_to_all(a, axes, split_axis=0, concat_axis=0, tiled=True)  4.8 us
    unnamed x15, local copies, waits for them, and re-layouts  4.13 us
  transfers between devices with their start and end apart: 8, of which 3 were waited for; matrix products, arithmetic and copies ran while one was open for 0% of the time, Pallas kernels for 2%

profile of v3, /device:TPU:4, one launch (start us, length us, event | category | flops | bytes accessed | tf_op | source)
XLA Modules:
  0.0 151.1 jit_solution(17047477245858172454)
XLA Ops:
  0.6 0.1 pad_add_fusion.pos_ref
  0.7 1.3 pad_maximum_fusion.xg_ref
  2.1 2.2 %shard_map.86 = (bf16[2,48,1536]{2,1,0:T(8,128)(2,1)S(1)}, bf16[2,48,1536]{2,1,0:T(8,128)(2,1)S(1)}, bf16[2,48,1536]{2,1,0:T(8,128)(2,1)S(1)}, bf16[2,48,1536]{2...) custom-call(s32[2]{0:T(128)S(1)} %pad_add_fusion.pos_ref, ...), custom_call_target="tpu_custom_call" | custom-call | flops 301989888 | bytes 3147272 | tf_op jit(solution)/shard_map/pallas_call | solution.py:41
  4.3 1.9 %collective-permute-start = (bf16[2,48,1536]{2,1,0:T(8,128)(2,1)S(1)}, bf16[2,48,1536]{2,1,0:T(8,128)(2,1)S(1)}, u32[]{:S(2)}, u32[]{:S(2)}) collective-permute-start(bf16[2,48,1536]{2,1,0:T(8,128)(2,1)S(1)} %get-tuple-element.13), channel_id=1, source_target_pairs={{0,64},{64,0},{128,192},{192,128},{256,320},{320,256},{384,448},{4... | collective-permute-start | bytes 884744 | tf_op jit(solution)/shard_map/ppermute | solution.py:237
  6.2 3.8 %collective-permute-start.1 = (bf16[2,48,1536]{2,1,0:T(8,128)(2,1)S(1)}, bf16[2,48,1536]{2,1,0:T(8,128)(2,1)S(1)}, u32[]{:S(2)}, u32[]{:S(2)}) collective-permute-start(bf16[2,48,1536]{2,1,0:T(8,128)(2,1)S(1)} %get-tuple-element.14), channel_id=1, source_target_pairs={{0,128},{64,192},{128,256},{192,320},{256,384},{320,448},{384,4},{... | collective-permute-start | bytes 884744 | tf_op jit(solution)/shard_map/ppermute | solution.py:237
  10.0 9.5 %collective-permute-start.2 = (bf16[2,48,1536]{2,1,0:T(8,128)(2,1)S(1)}, bf16[2,48,1536]{2,1,0:T(8,128)(2,1)S(1)}, u32[]{:S(2)}, u32[]{:S(2)}) collective-permute-start(bf16[2,48,1536]{2,1,0:T(8,128)(2,1)S(1)} %get-tuple-element.15), channel_id=1, source_target_pairs={{0,396},{64,460},{128,0},{192,64},{256,128},{320,192},{384,256},{4... | collective-permute-start | bytes 884744 | tf_op jit(solution)/shard_map/ppermute | solution.py:237
  19.5 1.9 %collective-permute-start.3 = (bf16[2,48,1536]{2,1,0:T(8,128)(2,1)S(1)}, bf16[2,48,1536]{2,1,0:T(8,128)(2,1)S(1)}, u32[]{:S(2)}, u32[]{:S(2)}) collective-permute-start(bf16[2,48,1536]{2,1,0:T(8,128)(2,1)S(1)} %get-tuple-element.16), channel_id=1, source_target_pairs={{0,192},{64,128},{128,320},{192,256},{256,448},{320,384},{384,68},... | collective-permute-start | bytes 884744 | tf_op jit(solution)/shard_map/ppermute | solution.py:237
  21.4 4.9 %collective-permute-start.4 = (bf16[2,48,1536]{2,1,0:T(8,128)(2,1)S(1)}, bf16[2,48,1536]{2,1,0:T(8,128)(2,1)S(1)}, u32[]{:S(2)}, u32[]{:S(2)}) collective-permute-start(bf16[2,48,1536]{2,1,0:T(8,128)(2,1)S(1)} %get-tuple-element.17), channel_id=1, source_target_pairs={{0,460},{64,396},{128,64},{192,0},{256,192},{320,128},{384,320},{4... | collective-permute-start | bytes 884744 | tf_op jit(solution)/shard_map/ppermute | solution.py:237
  26.3 1.9 %collective-permute-start.5 = (bf16[2,48,1536]{2,1,0:T(8,128)(2,1)}, bf16[2,48,1536]{2,1,0:T(8,128)(2,1)}, u32[]{:S(2)}, u32[]{:S(2)}) collective-permute-start(bf16[2,48,1536]{2,1,0:T(8,128)(2,1)} %get-tuple-element.18), channel_id=1, source_target_pairs={{0,256},{64,320},{128,384},{192,448},{256,4},{320,68},{384,132},{4... | collective-permute-start | bytes 884744 | tf_op jit(solution)/shard_map/ppermute | solution.py:237
  28.3 5.6 %collective-permute-start.6 = (bf16[2,48,1536]{2,1,0:T(8,128)(2,1)S(1)}, bf16[2,48,1536]{2,1,0:T(8,128)(2,1)}, u32[]{:S(2)}, u32[]{:S(2)}) collective-permute-start(bf16[2,48,1536]{2,1,0:T(8,128)(2,1)S(1)} %get-tuple-element.19), channel_id=1, source_target_pairs={{0,332},{64,268},{128,460},{192,396},{256,64},{320,0},{384,192},{4... | collective-permute-start | bytes 884744 | tf_op jit(solution)/shard_map/ppermute | solution.py:237
  33.9 0.0 copy-start.3
  33.9 1.3 copy-done.3
  35.2 1.5 %shard_map.87 = bf16[288,1152]{1,0:T(8,128)(2,1)S(1)} custom-call(bf16[2,48,1536]{2,1,0:T(8,128)(2,1)S(1)} %get-tuple-element.12.refs_0_, bf16[2,48,1536]{2,1,0:T(8,128)(2,1)S(1)} %collective-permute-done.refs_1_, bf16[2,48,1536]{2,1,0:T(8,128)(2,1)S(1)} %collective-permute-done.1.refs_2_, bf16[2,48,1536]{2,1,0:T(8,128)(2,1)S(1)} %collective-permute-done.2.refs_3_, ...), custom_call_target="tpu_custom_call" | custom-call | flops 1019215872 | bytes 5971968 | tf_op jit(solution)/shard_map/pallas_call | solution.py:41
  36.7 0.8 copy-done.2
  37.5 4.8 %all-to-all-start = ((bf16[4,72,1152]{2,1,0:T(8,128)(2,1)}), bf16[4,72,1152]{2,1,0:T(8,128)(2,1)S(1)}, u32[]{:S(2)}, u32[]{:S(2)}) async-start(bf16[4,72,1152]{2,1,0:T(8,128)(2,1)} %bitcast.16), calls=%async_computation | async-start | bytes 1327104 | tf_op jit(solution)/shard_map/all_to_all | solution.py:204
  42.3 1.9 %collective-permute-done.5.refs_0_ = bf16[2,48,1536]{2,1,0:T(8,128)(2,1)} collective-permute-done((bf16[2,48,1536]{2,1,0:T(8,128)(2,1)}, bf16[2,48,1536]{2,1,0:T(8,128)(2,1)}, u32[]{:S(2)}, u32[]{:S(2)}) %collective-permute-start.5) | collective-permute-done | bytes 294944 | tf_op jit(solution)/shard_map/ppermute | solution.py:237
  44.3 0.9 collective-permute-done.6.refs_1_
  45.2 1.3 copy-done.4
  46.5 2.2 %shard_map.88.a_ref = bf16[96,1152]{1,0:T(8,128)(2,1)S(1)} custom-call(bf16[2,48,1536]{2,1,0:T(8,128)(2,1)} %collective-permute-done.5.refs_0_, bf16[2,48,1536]{2,1,0:T(8,128)(2,1)} %collective-permute-done.6.refs_1_, bf16[384,1536]{1,0:T(8,128)(2,1)S(1)} %bitcast.11, bf16[384,1536]{1,0:T(8,128)(2,1)S(1)} %bitcast.14, bf16[384,1536]{1,0:T(8,128)(2,1)S(1)} %bitcast.19), custom_call_target="tpu_custom_call" | custom-call | flops 3397386240 | bytes 4349952 | tf_op jit(solution)/shard_map/pallas_call | solution.py:41
  48.6 2.4 %all-to-all-done._.refs_0_ = bf16[4,72,1152]{2,1,0:T(8,128)(2,1)S(1)} async-done(((bf16[4,72,1152]{2,1,0:T(8,128)(2,1)}), bf16[4,72,1152]{2,1,0:T(8,128)(2,1)S(1)}, u32[]{:S(2)}, u32[]{:S(2)}) %all-to-all-start) | async-done | bytes 663584 | tf_op jit(solution)/shard_map/all_to_all | solution.py:204
  51.1 9.2 %all_to_all.20.refs_1_ = bf16[4,24,1152]{2,1,0:T(8,128)(2,1)S(1)} all-to-all(bf16[4,24,1152]{2,1,0:T(8,128)(2,1)S(1)} %bitcast.20), channel_id=1, replica_groups=mesh['zl'=4,'c'=2,'y'=4,'zh'=4,'x'=4] {'x'}, dimensions={0} | all-to-all | bytes 442368 | tf_op jit(solution)/shard_map/all_to_all | solution.py:204
  60.3 0.2 shard_map.90
  60.5 14.0 %all_gather.12.d_ref = bf16[384,896]{1,0:T(8,128)(2,1)S(1)} all-gather(bf16[96,896]{1,0:T(8,128)(2,1)S(1)} %shard_map.90), channel_id=1, replica_groups=mesh['zl'=4,'c'=2,'y'=4,'zh'=4,'x'=4] {'x'}, dimensions={0}, use_global_device_ids=true | all-gather | bytes 860160 | tf_op jit(solution)/shard_map/all_gather | solution.py:257
  74.5 1.8 %shard_map.91 = bf16[4,400,384]{2,1,0:T(8,128)(2,1)S(1)} custom-call(bf16[384,896]{1,0:T(8,128)(2,1)S(1)} %all_gather.12.d_ref, bf16[384,1536]{1,0:T(8,128)(2,1)S(1)} %bitcast.12, bf16[384,1536]{1,0:T(8,128)(2,1)S(1)} %bitcast.15), custom_call_target="tpu_custom_call" | custom-call | flops 905969664 | bytes 4276224 | tf_op jit(solution)/shard_map/pallas_call | solution.py:41
  76.4 18.3 %all_to_all.21.part_ref = bf16[4,400,384]{2,1,0:T(8,128)(2,1)S(1)} all-to-all(bf16[4,400,384]{2,1,0:T(8,128)(2,1)S(1)} %shard_map.91), channel_id=1, replica_groups=mesh['zl'=4,'c'=2,'y'=4,'zh'=4,'x'=4] {'y'}, dimensions={0} | all-to-all | bytes 2457600 | tf_op jit(solution)/shard_map/all_to_all | solution.py:204
  94.7 0.7 shard_map.92
  95.4 13.9 %all_to_all.22.back_ref = bf16[8,56,384]{2,1,0:T(8,128)(2,1)S(1)} all-to-all(bf16[8,56,384]{2,1,0:T(8,128)(2,1)S(1)} %shard_map.92), channel_id=1, replica_groups=mesh['zl'=4,'c'=2,'y'=4,'zh'=4,'x'=4] {'zl','c'}, dimensions={0} | all-to-all | bytes 688128 | tf_op jit(solution)/shard_map/all_to_all | solution.py:204
  109.3 0.4 shard_map.93
  109.6 26.9 %all-gather = bf16[576,384]{1,0:T(8,128)(2,1)S(1)} all-gather(bf16[144,384]{1,0:T(8,128)(2,1)S(1)} %shard_map.93), channel_id=2, replica_groups=mesh['zl'=4,'c'=2,'y'=4,'zh'=4,'x'=4] {'zh'}, dimensions={0}, use_global_device_ids=true | all-gather | bytes 552960 | tf_op jit(solution)/shard_map/all_gather | solution.py:278
  136.5 0.6 shard_map.94
  137.1 13.3 %all_gather.15 = bf16[128,1536]{1,0:T(8,128)(2,1)S(1)} all-gather(bf16[128,384]{1,0:T(8,128)(2,1)S(1)} %get-tuple-element.20), channel_id=1, replica_groups=mesh['zl'=4,'c'=2,'y'=4,'zh'=4,'x'=4] {'y'}, dimensions={1}, use_global_device_ids=true | all-gather | bytes 491520 | tf_op jit(solution)/shard_map/all_gather | solution.py:281
  150.4 0.7 copy.10
  (16 shorter events, 0.0 us)
Async XLA Ops:
  0.6 1.4 copy-start.5
  0.7 33.1 %copy-start = (bf16[1,384,1536]{2,1,0:T(8,128)(2,1)S(1)}, bf16[1,384,1536]{2,1,0:T(8,128)(2,1)}, u32[]{:S(2)}) copy-start(bf16[1,384,1536]{2,1,0:T(8,128)(2,1)} %param.11) | copy-start | bytes 3538948
  0.7 33.2 %copy-start.1 = (bf16[1,384,1536]{2,1,0:T(8,128)(2,1)S(1)}, bf16[1,384,1536]{2,1,0:T(8,128)(2,1)}, u32[]{:S(2)}) copy-start(bf16[1,384,1536]{2,1,0:T(8,128)(2,1)} %param.12) | copy-start | bytes 3538948
  4.3 22.0 %collective-permute-start = (bf16[2,48,1536]{2,1,0:T(8,128)(2,1)S(1)}, bf16[2,48,1536]{2,1,0:T(8,128)(2,1)S(1)}, u32[]{:S(2)}, u32[]{:S(2)}) collective-permute-start(bf16[2,48,1536]{2,1,0:T(8,128)(2,1)S(1)} %get-tuple-element.13), channel_id=1, source_target_pairs={{0,64},{64,0},{128,192},{192,128},{256,320},{320,256},{384,448},{4... | collective-permute-start | bytes 884744 | tf_op jit(solution)/shard_map/ppermute | solution.py:237
  6.2 22.1 %collective-permute-start.1 = (bf16[2,48,1536]{2,1,0:T(8,128)(2,1)S(1)}, bf16[2,48,1536]{2,1,0:T(8,128)(2,1)S(1)}, u32[]{:S(2)}, u32[]{:S(2)}) collective-permute-start(bf16[2,48,1536]{2,1,0:T(8,128)(2,1)S(1)} %get-tuple-element.14), channel_id=1, source_target_pairs={{0,128},{64,192},{128,256},{192,320},{256,384},{320,448},{384,4},{... | collective-permute-start | bytes 884744 | tf_op jit(solution)/shard_map/ppermute | solution.py:237
  10.0 23.8 %collective-permute-start.2 = (bf16[2,48,1536]{2,1,0:T(8,128)(2,1)S(1)}, bf16[2,48,1536]{2,1,0:T(8,128)(2,1)S(1)}, u32[]{:S(2)}, u32[]{:S(2)}) collective-permute-start(bf16[2,48,1536]{2,1,0:T(8,128)(2,1)S(1)} %get-tuple-element.15), channel_id=1, source_target_pairs={{0,396},{64,460},{128,0},{192,64},{256,128},{320,192},{384,256},{4... | collective-permute-start | bytes 884744 | tf_op jit(solution)/shard_map/ppermute | solution.py:237
  19.5 14.3 %collective-permute-start.3 = (bf16[2,48,1536]{2,1,0:T(8,128)(2,1)S(1)}, bf16[2,48,1536]{2,1,0:T(8,128)(2,1)S(1)}, u32[]{:S(2)}, u32[]{:S(2)}) collective-permute-start(bf16[2,48,1536]{2,1,0:T(8,128)(2,1)S(1)} %get-tuple-element.16), channel_id=1, source_target_pairs={{0,192},{64,128},{128,320},{192,256},{256,448},{320,384},{384,68},... | collective-permute-start | bytes 884744 | tf_op jit(solution)/shard_map/ppermute | solution.py:237
  21.4 12.4 %collective-permute-start.4 = (bf16[2,48,1536]{2,1,0:T(8,128)(2,1)S(1)}, bf16[2,48,1536]{2,1,0:T(8,128)(2,1)S(1)}, u32[]{:S(2)}, u32[]{:S(2)}) collective-permute-start(bf16[2,48,1536]{2,1,0:T(8,128)(2,1)S(1)} %get-tuple-element.17), channel_id=1, source_target_pairs={{0,460},{64,396},{128,64},{192,0},{256,192},{320,128},{384,320},{4... | collective-permute-start | bytes 884744 | tf_op jit(solution)/shard_map/ppermute | solution.py:237
  26.3 17.9 %collective-permute-start.5 = (bf16[2,48,1536]{2,1,0:T(8,128)(2,1)}, bf16[2,48,1536]{2,1,0:T(8,128)(2,1)}, u32[]{:S(2)}, u32[]{:S(2)}) collective-permute-start(bf16[2,48,1536]{2,1,0:T(8,128)(2,1)} %get-tuple-element.18), channel_id=1, source_target_pairs={{0,256},{64,320},{128,384},{192,448},{256,4},{320,68},{384,132},{4... | collective-permute-start | bytes 884744 | tf_op jit(solution)/shard_map/ppermute | solution.py:237
  28.3 16.9 %collective-permute-start.6 = (bf16[2,48,1536]{2,1,0:T(8,128)(2,1)S(1)}, bf16[2,48,1536]{2,1,0:T(8,128)(2,1)}, u32[]{:S(2)}, u32[]{:S(2)}) collective-permute-start(bf16[2,48,1536]{2,1,0:T(8,128)(2,1)S(1)} %get-tuple-element.19), channel_id=1, source_target_pairs={{0,332},{64,268},{128,460},{192,396},{256,64},{320,0},{384,192},{4... | collective-permute-start | bytes 884744 | tf_op jit(solution)/shard_map/ppermute | solution.py:237
  33.9 1.3 copy-start.3
  36.7 0.8 copy-start.2
  37.5 13.5 %all-to-all-start = ((bf16[4,72,1152]{2,1,0:T(8,128)(2,1)}), bf16[4,72,1152]{2,1,0:T(8,128)(2,1)S(1)}, u32[]{:S(2)}, u32[]{:S(2)}) async-start(bf16[4,72,1152]{2,1,0:T(8,128)(2,1)} %bitcast.16), calls=%async_computation | async-start | bytes 1327104 | tf_op jit(solution)/shard_map/all_to_all | solution.py:204
  45.2 1.3 copy-start.4
  94.7 14.6 %copy-start.6 = (bf16[8,48]{1,0:T(8,128)(2,1)S(1)}, bf16[8,48]{1,0:T(8,128)(2,1)}, u32[]{:S(2)}) copy-start(bf16[8,48]{1,0:T(8,128)(2,1)} %weights_ref.1) | copy-start | bytes 2308

commit v4 on v3

--- a/solution.py
+++ b/solution.py
@@ -52,7 +52,7 @@
 BLOCKS = ((0, 0), (0, 1), (1, 0), (-1, 0), (1, 1), (-1, 1), (2, 0), (-2, 1))
 NEAR = 6
 NEAR_COST, FAR_COST = 1, 10
-SENT = (2, 3, 4, 5, 1, 6, 7)
+SENT = (2, 3, 4, 5, 6, 7)
 
 
 def at(pos_ref, dz, dc):
@@ -86,9 +86,10 @@
     out_ref[...] = a_ref[...]
 
 
-def forward_kernel(*refs):
+def forward_kernel(pos_ref, *refs):
     blocks, (gate_ref, up_ref, down_ref, out_ref, x_ref, g_ref) = refs[:-6], refs[-6:]
     taken = blocks[0].shape[1]
+    blocks = [ref if len(ref.shape) == 3 else ref.at[1 - pos_ref[1]] for ref in blocks]
     for which, rows_ref in enumerate((x_ref, g_ref)):
         for i, block in enumerate(blocks):
             rows_ref[i * taken : (i + 1) * taken, :] = block[which]
@@ -235,13 +236,15 @@
     got = {0: sent[0]}
     for i in SENT:
         got[i] = lax.ppermute(sent[i], RING, along_z(*BLOCKS[i]))
+    got[1] = lax.all_gather(sent[1], "c")
 
     def project(blocks, factor):
         count = len(blocks) * taken
         return call(
             forward_kernel,
             sds((count, 3 * hidden)),
-            (*blocks, w_gate, w_up, w_down),
+            (pos, *blocks, w_gate, w_up, w_down),
+            specs=[SMEM] + [VMEM] * (len(blocks) + 3),
             flops=int(factor * 6 * count * hidden * width),
             scratch=[pltpu.VMEM((count, width), BF16)] * 2,
         )

time: 152 us -> 150 us (0.987)
  starting transfers between devices: 34.3 us -> 31.7 us
  blocking collectives: 95.5 us -> 97.8 us
    all_gather x0 -> x1, blocking collectives: none -> 3.09 us  [local(): got[1] = lax.all_gather(sent[1], 'c')]
    ppermute x7 -> x6, starting transfers between devices: 29.5 us -> 26.9 us  [local(): got[i] = lax.ppermute(sent[i], RING, along_z(*BLOCKS[i]))]
    ppermute x7 -> x6, waiting for transfers between devices: 2.85 us -> 0.53 us  [local(): got[i] = lax.ppermute(sent[i], RING, along_z(*BLOCKS[i]))]
    all_to_all x1, waiting for transfers between devices: 2.44 us -> 4.55 us  [exchange(): return lax.all_to_all(a, axes, split_axis=0, concat_axis=0, tiled=True)]
  transfers between devices with their start and end apart: 8 -> 7, of which waited for: 3 -> 2; matrix products, arithmetic and copies ran while one was open for 0% -> 0% of each run, Pallas kernels for 2% -> 3%
where the time goes in v4:
time: 150 us
  blocking collectives  97.8 us (65%)
  starting transfers between devices  31.7 us (21%)
  Pallas kernels  10.2 us (7%)
  waiting for transfers between devices  5.08 us (3%)
  local copies, waits for them, and re-layouts  2.88 us (2%)
    all_to_all x3, blocking collectives, exchange(): return lax.all_to_all(a, axes, split_axis=0, concat_axis=0, tiled=True)  41.3 us
    ppermute x6, starting transfers between devices, local(): got[i] = lax.ppermute(sent[i], RING, along_z(*BLOCKS[i]))  26.9 us
    all_gather x1, blocking collectives, local(): lax.all_gather(mine, 'zh')  26.3 us
    all_gather x1, blocking collectives, local(): d = lax.all_gather(d_block, 'x', tiled=True)  13.8 us
    all_gather x1, blocking collectives, local(): return (lax.all_gather(token_grad, 'y', axis=1, tiled=True), score_grad)  13.4 us
    pallas_call x9, Pallas kernels, call(): pl.pallas_call(kernel, out_shape=outs, in_specs=specs or [VMEM] * len(arg...  10.2 us
    all_to_all x1, starting transfers between devices, exchange(): return lax.all_to_all(a, axes, split_axis=0, concat_axis=0, tiled=True)  4.81 us
    all_to_all x1, waiting for transfers between devices, exchange(): return lax.all_to_all(a, axes, split_axis=0, concat_axis=0, tiled=True)  4.55 us
  transfers between devices with their start and end apart: 7, of which 2 were waited for; matrix products, arithmetic and copies ran while one was open for 0% of the time, Pallas kernels for 3%

profile of v4, /device:TPU:4, one launch (start us, length us, event | category | flops | bytes accessed | tf_op | source)
XLA Modules:
  0.0 149.9 jit_solution(3045148196879677922)
XLA Ops:
  0.6 0.1 pad_add_fusion.pos_ref
  0.7 1.3 pad_maximum_fusion.xg_ref
  2.1 0.0 copy-start
  2.1 2.2 %shard_map.86 = (bf16[2,48,1536]{2,1,0:T(8,128)(2,1)S(1)}, bf16[2,48,1536]{2,1,0:T(8,128)(2,1)S(1)}, bf16[2,48,1536]{2,1,0:T(8,128)(2,1)S(1)}, bf16[2,48,1536]{2...) custom-call(s32[2]{0:T(128)S(1)} %pad_add_fusion.pos_ref, ...), custom_call_target="tpu_custom_call" | custom-call | flops 301989888 | bytes 3147272 | tf_op jit(solution)/shard_map/pallas_call | solution.py:41
  4.3 3.8 %collective-permute-start = (bf16[2,48,1536]{2,1,0:T(8,128)(2,1)S(1)}, bf16[2,48,1536]{2,1,0:T(8,128)(2,1)S(1)}, u32[]{:S(2)}, u32[]{:S(2)}) collective-permute-start(bf16[2,48,1536]{2,1,0:T(8,128)(2,1)S(1)} %get-tuple-element.14), channel_id=1, source_target_pairs={{0,128},{64,192},{128,256},{192,320},{256,384},{320,448},{384,4},{... | collective-permute-start | bytes 884744 | tf_op jit(solution)/shard_map/ppermute | solution.py:238
  8.1 9.5 %collective-permute-start.1 = (bf16[2,48,1536]{2,1,0:T(8,128)(2,1)S(1)}, bf16[2,48,1536]{2,1,0:T(8,128)(2,1)S(1)}, u32[]{:S(2)}, u32[]{:S(2)}) collective-permute-start(bf16[2,48,1536]{2,1,0:T(8,128)(2,1)S(1)} %get-tuple-element.15), channel_id=1, source_target_pairs={{0,396},{64,460},{128,0},{192,64},{256,128},{320,192},{384,256},{4... | collective-permute-start | bytes 884744 | tf_op jit(solution)/shard_map/ppermute | solution.py:238
  17.6 1.9 %collective-permute-start.2 = (bf16[2,48,1536]{2,1,0:T(8,128)(2,1)S(1)}, bf16[2,48,1536]{2,1,0:T(8,128)(2,1)S(1)}, u32[]{:S(2)}, u32[]{:S(2)}) collective-permute-start(bf16[2,48,1536]{2,1,0:T(8,128)(2,1)S(1)} %get-tuple-element.16), channel_id=1, source_target_pairs={{0,192},{64,128},{128,320},{192,256},{256,448},{320,384},{384,68},... | collective-permute-start | bytes 884744 | tf_op jit(solution)/shard_map/ppermute | solution.py:238
  19.5 4.9 %collective-permute-start.3 = (bf16[2,48,1536]{2,1,0:T(8,128)(2,1)S(1)}, bf16[2,48,1536]{2,1,0:T(8,128)(2,1)S(1)}, u32[]{:S(2)}, u32[]{:S(2)}) collective-permute-start(bf16[2,48,1536]{2,1,0:T(8,128)(2,1)S(1)} %get-tuple-element.17), channel_id=1, source_target_pairs={{0,460},{64,396},{128,64},{192,0},{256,192},{320,128},{384,320},{4... | collective-permute-start | bytes 884744 | tf_op jit(solution)/shard_map/ppermute | solution.py:238
  24.4 1.9 %collective-permute-start.4 = (bf16[2,48,1536]{2,1,0:T(8,128)(2,1)}, bf16[2,48,1536]{2,1,0:T(8,128)(2,1)}, u32[]{:S(2)}, u32[]{:S(2)}) collective-permute-start(bf16[2,48,1536]{2,1,0:T(8,128)(2,1)} %get-tuple-element.18), channel_id=1, source_target_pairs={{0,256},{64,320},{128,384},{192,448},{256,4},{320,68},{384,132},{4... | collective-permute-start | bytes 884744 | tf_op jit(solution)/shard_map/ppermute | solution.py:238
  26.3 4.9 %collective-permute-start.5 = (bf16[2,48,1536]{2,1,0:T(8,128)(2,1)S(1)}, bf16[2,48,1536]{2,1,0:T(8,128)(2,1)}, u32[]{:S(2)}, u32[]{:S(2)}) collective-permute-start(bf16[2,48,1536]{2,1,0:T(8,128)(2,1)S(1)} %get-tuple-element.19), channel_id=1, source_target_pairs={{0,332},{64,268},{128,460},{192,396},{256,64},{320,0},{384,192},{4... | collective-permute-start | bytes 884744 | tf_op jit(solution)/shard_map/ppermute | solution.py:238
  31.2 3.1 %all-gather = bf16[4,48,1536]{2,1,0:T(8,128)(2,1)S(1)} all-gather(bf16[2,48,1536]{2,1,0:T(8,128)(2,1)S(1)} %get-tuple-element.13), channel_id=2, replica_groups=mesh['zl'=4,'c'=2,'y'=4,'zh'=4,'x'=4] {'c'}, dimensions={0}, use_global_device_ids=true | all-gather | bytes 884736 | tf_op jit(solution)/shard_map/all_gather | solution.py:239
  34.3 0.0 collective-permute-done.1.refs_3_
  34.4 2.1 %shard_map.87 = bf16[288,1152]{1,0:T(8,128)(2,1)S(1)} custom-call(s32[2]{0:T(128)S(1)} %pad_add_fusion.pos_ref, bf16[2,48,1536]{2,1,0:T(8,128)(2,1)S(1)} %get-tuple-element.12.refs_0_, bf16[2,2,48,1536]{3,2,1,0:T(8,128)(2,1)S(1)} %bitcast.18, bf16[2,48,1536]{2,1,0:T(8,128)(2,1)S(1)} %collective-permute-done.refs_2_, ...), custom_call_target="tpu_custom_call" | custom-call | flops 1019215872 | bytes 6266888 | tf_op jit(solution)/shard_map/pallas_call | solution.py:41
  36.5 0.8 copy-done.2
  37.3 4.8 %all-to-all-start = ((bf16[4,72,1152]{2,1,0:T(8,128)(2,1)}), bf16[4,72,1152]{2,1,0:T(8,128)(2,1)S(1)}, u32[]{:S(2)}, u32[]{:S(2)}) async-start(bf16[4,72,1152]{2,1,0:T(8,128)(2,1)} %bitcast.17), calls=%async_computation | async-start | bytes 1327104 | tf_op jit(solution)/shard_map/all_to_all | solution.py:205
  42.1 0.0 collective-permute-done.4.refs_0_
  42.1 0.5 collective-permute-done.5.refs_1_
  42.6 1.3 copy-done.4
  43.9 2.2 %shard_map.88.a_ref = bf16[96,1152]{1,0:T(8,128)(2,1)S(1)} custom-call(s32[2]{0:T(128)S(1)} %pad_add_fusion.pos_ref, bf16[2,48,1536]{2,1,0:T(8,128)(2,1)} %collective-permute-done.4.refs_0_, bf16[2,48,1536]{2,1,0:T(8,128)(2,1)} %collective-permute-done.5.refs_1_, bf16[384,1536]{1,0:T(8,128)(2,1)S(1)} %bitcast.12, bf16[384,1536]{1,0:T(8,128)(2,1)S(1)} %bitcast.15, ...), custom_call_target="tpu_custom_call" | custom-call | flops 3397386240 | bytes 4349960 | tf_op jit(solution)/shard_map/pallas_call | solution.py:41
  46.1 4.5 %all-to-all-done._.refs_0_ = bf16[4,72,1152]{2,1,0:T(8,128)(2,1)S(1)} async-done(((bf16[4,72,1152]{2,1,0:T(8,128)(2,1)}), bf16[4,72,1152]{2,1,0:T(8,128)(2,1)S(1)}, u32[]{:S(2)}, u32[]{:S(2)}) %all-to-all-start) | async-done | bytes 663584 | tf_op jit(solution)/shard_map/all_to_all | solution.py:205
  50.7 9.2 %all_to_all.20.refs_1_ = bf16[4,24,1152]{2,1,0:T(8,128)(2,1)S(1)} all-to-all(bf16[4,24,1152]{2,1,0:T(8,128)(2,1)S(1)} %bitcast.22), channel_id=1, replica_groups=mesh['zl'=4,'c'=2,'y'=4,'zh'=4,'x'=4] {'x'}, dimensions={0} | all-to-all | bytes 442368 | tf_op jit(solution)/shard_map/all_to_all | solution.py:205
  59.9 0.2 shard_map.90
  60.1 13.8 %all_gather.20.d_ref = bf16[384,896]{1,0:T(8,128)(2,1)S(1)} all-gather(bf16[96,896]{1,0:T(8,128)(2,1)S(1)} %shard_map.90), channel_id=1, replica_groups=mesh['zl'=4,'c'=2,'y'=4,'zh'=4,'x'=4] {'x'}, dimensions={0}, use_global_device_ids=true | all-gather | bytes 860160 | tf_op jit(solution)/shard_map/all_gather | solution.py:260
  73.9 1.8 %shard_map.91 = bf16[4,400,384]{2,1,0:T(8,128)(2,1)S(1)} custom-call(bf16[384,896]{1,0:T(8,128)(2,1)S(1)} %all_gather.20.d_ref, bf16[384,1536]{1,0:T(8,128)(2,1)S(1)} %bitcast.13, bf16[384,1536]{1,0:T(8,128)(2,1)S(1)} %bitcast.16), custom_call_target="tpu_custom_call" | custom-call | flops 905969664 | bytes 4276224 | tf_op jit(solution)/shard_map/pallas_call | solution.py:41
  75.7 18.2 %all_to_all.21.part_ref = bf16[4,400,384]{2,1,0:T(8,128)(2,1)S(1)} all-to-all(bf16[4,400,384]{2,1,0:T(8,128)(2,1)S(1)} %shard_map.91), channel_id=1, replica_groups=mesh['zl'=4,'c'=2,'y'=4,'zh'=4,'x'=4] {'y'}, dimensions={0} | all-to-all | bytes 2457600 | tf_op jit(solution)/shard_map/all_to_all | solution.py:205
  93.9 0.7 shard_map.92
  94.6 13.9 %all_to_all.22.back_ref = bf16[8,56,384]{2,1,0:T(8,128)(2,1)S(1)} all-to-all(bf16[8,56,384]{2,1,0:T(8,128)(2,1)S(1)} %shard_map.92), channel_id=1, replica_groups=mesh['zl'=4,'c'=2,'y'=4,'zh'=4,'x'=4] {'zl','c'}, dimensions={0} | all-to-all | bytes 688128 | tf_op jit(solution)/shard_map/all_to_all | solution.py:205
  108.5 0.4 shard_map.93
  108.9 26.3 %all-gather.1 = bf16[576,384]{1,0:T(8,128)(2,1)S(1)} all-gather(bf16[144,384]{1,0:T(8,128)(2,1)S(1)} %shard_map.93), channel_id=3, replica_groups=mesh['zl'=4,'c'=2,'y'=4,'zh'=4,'x'=4] {'zh'}, dimensions={0}, use_global_device_ids=true | all-gather | bytes 552960 | tf_op jit(solution)/shard_map/all_gather | solution.py:281
  135.2 0.6 shard_map.94
  135.8 13.4 %all_gather.23 = bf16[128,1536]{1,0:T(8,128)(2,1)S(1)} all-gather(bf16[128,384]{1,0:T(8,128)(2,1)S(1)} %get-tuple-element.20), channel_id=1, replica_groups=mesh['zl'=4,'c'=2,'y'=4,'zh'=4,'x'=4] {'y'}, dimensions={1}, use_global_device_ids=true | all-gather | bytes 491520 | tf_op jit(solution)/shard_map/all_gather | solution.py:284
  149.2 0.7 copy.10
  (15 shorter events, 0.0 us)
Async XLA Ops:
  0.6 1.4 copy-start.5
  0.7 33.6 %copy-start.1 = (bf16[1,384,1536]{2,1,0:T(8,128)(2,1)S(1)}, bf16[1,384,1536]{2,1,0:T(8,128)(2,1)}, u32[]{:S(2)}) copy-start(bf16[1,384,1536]{2,1,0:T(8,128)(2,1)} %param.12) | copy-start | bytes 3538948
  0.7 33.6 %copy-start.3 = (bf16[1,384,1536]{2,1,0:T(8,128)(2,1)S(1)}, bf16[1,384,1536]{2,1,0:T(8,128)(2,1)}, u32[]{:S(2)}) copy-start(bf16[1,384,1536]{2,1,0:T(8,128)(2,1)} %param.13) | copy-start | bytes 3538948
  2.1 32.3 %copy-start = (bf16[1,384,1536]{2,1,0:T(8,128)(2,1)S(1)}, bf16[1,384,1536]{2,1,0:T(8,128)(2,1)}, u32[]{:S(2)}) copy-start(bf16[1,384,1536]{2,1,0:T(8,128)(2,1)} %param.11) | copy-start | bytes 3538948
  4.3 22.0 %collective-permute-start = (bf16[2,48,1536]{2,1,0:T(8,128)(2,1)S(1)}, bf16[2,48,1536]{2,1,0:T(8,128)(2,1)S(1)}, u32[]{:S(2)}, u32[]{:S(2)}) collective-permute-start(bf16[2,48,1536]{2,1,0:T(8,128)(2,1)S(1)} %get-tuple-element.14), channel_id=1, source_target_pairs={{0,128},{64,192},{128,256},{192,320},{256,384},{320,448},{384,4},{... | collective-permute-start | bytes 884744 | tf_op jit(solution)/shard_map/ppermute | solution.py:238
  8.1 26.2 %collective-permute-start.1 = (bf16[2,48,1536]{2,1,0:T(8,128)(2,1)S(1)}, bf16[2,48,1536]{2,1,0:T(8,128)(2,1)S(1)}, u32[]{:S(2)}, u32[]{:S(2)}) collective-permute-start(bf16[2,48,1536]{2,1,0:T(8,128)(2,1)S(1)} %get-tuple-element.15), channel_id=1, source_target_pairs={{0,396},{64,460},{128,0},{192,64},{256,128},{320,192},{384,256},{4... | collective-permute-start | bytes 884744 | tf_op jit(solution)/shard_map/ppermute | solution.py:238
  17.6 16.7 %collective-permute-start.2 = (bf16[2,48,1536]{2,1,0:T(8,128)(2,1)S(1)}, bf16[2,48,1536]{2,1,0:T(8,128)(2,1)S(1)}, u32[]{:S(2)}, u32[]{:S(2)}) collective-permute-start(bf16[2,48,1536]{2,1,0:T(8,128)(2,1)S(1)} %get-tuple-element.16), channel_id=1, source_target_pairs={{0,192},{64,128},{128,320},{192,256},{256,448},{320,384},{384,68},... | collective-permute-start | bytes 884744 | tf_op jit(solution)/shard_map/ppermute | solution.py:238
  19.5 14.8 %collective-permute-start.3 = (bf16[2,48,1536]{2,1,0:T(8,128)(2,1)S(1)}, bf16[2,48,1536]{2,1,0:T(8,128)(2,1)S(1)}, u32[]{:S(2)}, u32[]{:S(2)}) collective-permute-start(bf16[2,48,1536]{2,1,0:T(8,128)(2,1)S(1)} %get-tuple-element.17), channel_id=1, source_target_pairs={{0,460},{64,396},{128,64},{192,0},{256,192},{320,128},{384,320},{4... | collective-permute-start | bytes 884744 | tf_op jit(solution)/shard_map/ppermute | solution.py:238
  24.4 17.7 %collective-permute-start.4 = (bf16[2,48,1536]{2,1,0:T(8,128)(2,1)}, bf16[2,48,1536]{2,1,0:T(8,128)(2,1)}, u32[]{:S(2)}, u32[]{:S(2)}) collective-permute-start(bf16[2,48,1536]{2,1,0:T(8,128)(2,1)} %get-tuple-element.18), channel_id=1, source_target_pairs={{0,256},{64,320},{128,384},{192,448},{256,4},{320,68},{384,132},{4... | collective-permute-start | bytes 884744 | tf_op jit(solution)/shard_map/ppermute | solution.py:238
  26.3 16.3 %collective-permute-start.5 = (bf16[2,48,1536]{2,1,0:T(8,128)(2,1)S(1)}, bf16[2,48,1536]{2,1,0:T(8,128)(2,1)}, u32[]{:S(2)}, u32[]{:S(2)}) collective-permute-start(bf16[2,48,1536]{2,1,0:T(8,128)(2,1)S(1)} %get-tuple-element.19), channel_id=1, source_target_pairs={{0,332},{64,268},{128,460},{192,396},{256,64},{320,0},{384,192},{4... | collective-permute-start | bytes 884744 | tf_op jit(solution)/shard_map/ppermute | solution.py:238
  36.5 0.8 copy-start.2
  37.3 13.3 %all-to-all-start = ((bf16[4,72,1152]{2,1,0:T(8,128)(2,1)}), bf16[4,72,1152]{2,1,0:T(8,128)(2,1)S(1)}, u32[]{:S(2)}, u32[]{:S(2)}) async-start(bf16[4,72,1152]{2,1,0:T(8,128)(2,1)} %bitcast.17), calls=%async_computation | async-start | bytes 1327104 | tf_op jit(solution)/shard_map/all_to_all | solution.py:205
  42.6 1.3 copy-start.4
  93.9 14.6 %copy-start.6 = (bf16[8,48]{1,0:T(8,128)(2,1)S(1)}, bf16[8,48]{1,0:T(8,128)(2,1)}, u32[]{:S(2)}) copy-start(bf16[8,48]{1,0:T(8,128)(2,1)} %weights_ref.1) | copy-start | bytes 2308

commit v5 on v3

--- a/solution.py
+++ b/solution.py
@@ -17,7 +17,6 @@
 SIZES = {"zl": 4, "c": 2, "y": 4, "zh": 4, "x": 4}
 LIMIT = 16
 VMEM = pl.BlockSpec(memory_space=pltpu.VMEM)
-SMEM = pl.BlockSpec(memory_space=pltpu.SMEM)
 
 
 def dot(a, b, ca, cb):
@@ -52,22 +51,22 @@
 BLOCKS = ((0, 0), (0, 1), (1, 0), (-1, 0), (1, 1), (-1, 1), (2, 0), (-2, 1))
 NEAR = 6
 NEAR_COST, FAR_COST = 1, 10
-SENT = (2, 3, 4, 5, 1, 6, 7)
-
-
-def at(pos_ref, dz, dc):
+SENT = (2, 3, 4, 5, 6, 7)
+
+
+def at(dz, dc):
     chips, cores = SIZES["zl"], SIZES["c"]
-    return lax.rem(pos_ref[0] + (dz + chips), chips) * cores + lax.rem(pos_ref[1] + dc, cores)
-
-
-def pick_kernel(pos_ref, picks_ref, xg_ref, *refs):
+    return lax.rem(lax.axis_index("zl") + (dz + chips), chips) * cores + lax.rem(lax.axis_index("c") + dc, cores)
+
+
+def pick_kernel(picks_ref, xg_ref, *refs):
     *outs, hot_ref = refs
     experts, taken = picks_ref.shape
     tokens, width = xg_ref.shape[1:]
     row = iota(picks_ref.shape, 0)
     values = picks_ref[...].astype(F32)
     picked = [
-        jnp.sum(jnp.where(row == at(pos_ref, *b), values, 0.0), axis=0, keepdims=True) for b in BLOCKS
+        jnp.sum(jnp.where(row == at(*b), values, 0.0), axis=0, keepdims=True) for b in BLOCKS
     ]
     picks = jnp.transpose(jnp.concatenate(picked, axis=0))
     lane = iota((taken, tokens), 1).astype(F32)
@@ -89,6 +88,7 @@
 def forward_kernel(*refs):
     blocks, (gate_ref, up_ref, down_ref, out_ref, x_ref, g_ref) = refs[:-6], refs[-6:]
     taken = blocks[0].shape[1]
+    blocks = [ref if len(ref.shape) == 3 else ref.at[1 - lax.axis_index("c")] for ref in blocks]
     for which, rows_ref in enumerate((x_ref, g_ref)):
         for i, block in enumerate(blocks):
             rows_ref[i * taken : (i + 1) * taken, :] = block[which]
@@ -152,25 +152,31 @@
         out_ref[k, rows:, :LANES] = block
 
 
-def sum_kernel(pos_ref, part_ref, out_ref):
+def sum_kernel(part_ref, out_ref, rows_ref):
     parts, _, share = part_ref.shape
     shards, each, _ = out_ref.shape
     each -= TAIL
     rows = shards * each
-    total = add_up([part_ref[k].astype(F32) for k in range(parts)])
     one = rows // SIZES["x"]
     near = one * NEAR // len(BLOCKS)
-    ordered = [total[x * one : x * one + near] for x in range(SIZES["x"])]
-    ordered += [total[x * one + near : (x + 1) * one] for x in range(SIZES["x"])]
-    ordered = jnp.concatenate(ordered, axis=0)
-    score = total[rows : rows + shards] + total[rows + shards :]
+
+    def total(start, count):
+        return add_up([part_ref[k, start : start + count, :].astype(F32) for k in range(parts)])
+
+    for x in range(SIZES["x"]):
+        mine = total(x * one, one)
+        rows_ref[x * near : (x + 1) * near, :] = mine[:near]
+        far = SIZES["x"] * near + x * (one - near)
+        rows_ref[far : far + one - near, :] = mine[near:]
+    score = total(rows, PAD)
+    score = score[:shards] + score[shards:]
     high = score.astype(BF16).astype(F32)
     low = score - high
     row = iota((TAIL, share), 0)
     for i, (dz, dc) in enumerate(BLOCKS):
         both = jnp.where(row == 0, high[i : i + 1], jnp.where(row == 1, low[i : i + 1], 0.0))
-        block = jnp.concatenate([ordered[i * each : (i + 1) * each], both], axis=0)
-        out_ref[at(pos_ref, -dz, dc)] = block.astype(BF16)
+        block = jnp.concatenate([rows_ref[i * each : (i + 1) * each, :], both], axis=0)
+        out_ref[at(-dz, dc)] = block.astype(BF16)
 
 
 def scatter_kernel(picks_ref, weights_ref, back_ref, out_ref):
@@ -191,12 +197,18 @@
     out_ref[tokens:, :] = scores.astype(BF16)
 
 
-def final_kernel(part_ref, grad_ref, score_ref):
-    tokens = grad_ref.shape[0]
+def token_kernel(part_ref, out_ref):
+    tokens = out_ref.shape[0]
+    out_ref[...] = add_up([part_ref[k, :tokens, :].astype(F32) for k in range(part_ref.shape[0])]).astype(BF16)
+
+
+def final_kernel(gathered_ref, part_ref, grad_ref, score_ref):
+    parts, tokens, share = gathered_ref.shape
     experts, taken = score_ref.shape
-    total = add_up([part_ref[k].astype(F32) for k in range(part_ref.shape[0])])
-    grad_ref[...] = total[:tokens].astype(BF16)
-    score = total[tokens : tokens + experts] + total[tokens + experts :]
+    for k in range(parts):
+        grad_ref[:, k * share : (k + 1) * share] = gathered_ref[k]
+    total = add_up([part_ref[k, tokens:, :].astype(F32) for k in range(part_ref.shape[0])])
+    score = total[:experts] + total[experts:]
     score_ref[...] = score[:, :taken].astype(BF16)
 
 
@@ -223,18 +235,17 @@
     ny, nx = SIZES["y"], SIZES["x"]
     share, block = width // ny, rows // nx
 
-    pos = jnp.stack([lax.axis_index(a).astype(jnp.int32) for a in EXPERT])
     sent = call(
         pick_kernel,
         [sds((2, taken, width))] * experts,
-        (pos, picks, jnp.stack([layer_input, out_grad])),
+        (picks, jnp.stack([layer_input, out_grad])),
         flops=4 * rows * tokens * width,
-        specs=[SMEM, VMEM, VMEM],
         scratch=[pltpu.VMEM((rows, tokens), BF16)],
     )
     got = {0: sent[0]}
     for i in SENT:
         got[i] = lax.ppermute(sent[i], RING, along_z(*BLOCKS[i]))
+    got[1] = lax.all_gather(sent[1], "c")
 
     def project(blocks, factor):
         count = len(blocks) * taken
@@ -264,21 +275,22 @@
     summed = call(
         sum_kernel,
         sds((experts, taken + TAIL, share)),
-        (pos, exchange(part, "y")),
+        (exchange(part, "y"),),
         flops=4 * part.size,
-        specs=[SMEM, VMEM],
+        scratch=[pltpu.VMEM((rows, share), F32)],
     )
     back = exchange(summed, EXPERT)
     mine = call(
         scatter_kernel, sds((tokens + PAD, share)), (picks, scores, back), flops=2 * rows * tokens * share
     )
-    token_grad, score_grad = call(
+    over_zh = lax.all_gather(mine, "zh")
+    token_grad = call(token_kernel, sds((tokens, share)), (over_zh,), flops=4 * mine.size)
+    return call(
         final_kernel,
-        [sds((tokens, share)), sds((experts, taken))],
-        (lax.all_gather(mine, "zh"),),
-        flops=4 * mine.size,
-    )
-    return lax.all_gather(token_grad, "y", axis=1, tiled=True), score_grad
+        (sds((tokens, width)), sds((experts, taken))),
+        (lax.all_gather(token_grad, "y"), over_zh),
+        flops=0,
+    )
 
 
 def solution(mesh):

time: 152 us -> 148 us (0.974)
  starting transfers between devices: 34.3 us -> 31.7 us
  local copies, waits for them, and re-layouts: 4.13 us -> 2.14 us
  blocking collectives: 95.5 us -> 97.4 us
    ppermute x7 -> x6, starting transfers between devices: 29.5 us -> 26.9 us  [local(): got[i] = lax.ppermute(sent[i], RING, along_z(*BLOCKS[i]))]
    all_gather x2 -> x3, blocking collectives: 40.2 us -> 42.3 us  [the longest x1 26.3 us: local(): over_zh = lax.all_gather(mine, 'zh')]
    unnamed x15 -> x14, local copies, waits for them, and re-layouts: 4.13 us -> 2.14 us
    ppermute x7 -> x6, waiting for transfers between devices: 2.85 us -> 1.06 us  [local(): got[i] = lax.ppermute(sent[i], RING, along_z(*BLOCKS[i]))]
    all_to_all x1, waiting for transfers between devices: 2.44 us -> 4.02 us  [exchange(): return lax.all_to_all(a, axes, split_axis=0, concat_axis=0, tiled=True)]
    pallas_call x9 -> x10, Pallas kernels: 9.65 us -> 8.82 us  [call(): pl.pallas_call(kernel, out_shape=outs, in_specs=specs or [VMEM] * len(arg...]
  transfers between devices with their start and end apart: 8 -> 7, of which waited for: 3 -> 2; matrix products, arithmetic and copies ran while one was open for 0% -> 0% of each run, Pallas kernels for 2% -> 3%
where the time goes in v5:
time: 148 us; the launch traced here: 147 us
  blocking collectives  97.4 us (66%)
  starting transfers between devices  31.7 us (21%)
  Pallas kernels  8.82 us (6%)
  waiting for transfers between devices  5.08 us (3%)
  local copies, waits for them, and re-layouts  2.14 us (1%)
    all_to_all x3, blocking collectives, exchange(): return lax.all_to_all(a, axes, split_axis=0, concat_axis=0, tiled=True)  41.3 us
    ppermute x6, starting transfers between devices, local(): got[i] = lax.ppermute(sent[i], RING, along_z(*BLOCKS[i]))  26.9 us
    all_gather x1, blocking collectives, local(): over_zh = lax.all_gather(mine, 'zh')  26.3 us
    all_gather x1, blocking collectives, local(): d = lax.all_gather(d_block, 'x', tiled=True)  13.8 us
    all_gather x1, blocking collectives, local(): lax.all_gather(token_grad, 'y')  12.9 us
    pallas_call x10, Pallas kernels, call(): pl.pallas_call(kernel, out_shape=outs, in_specs=specs or [VMEM] * len(arg...  8.82 us
    all_to_all x1, starting transfers between devices, exchange(): return lax.all_to_all(a, axes, split_axis=0, concat_axis=0, tiled=True)  4.81 us
    all_to_all x1, waiting for transfers between devices, exchange(): return lax.all_to_all(a, axes, split_axis=0, concat_axis=0, tiled=True)  4.02 us
  transfers between devices with their start and end apart: 7, of which 2 were waited for; matrix products, arithmetic and copies ran while one was open for 0% of the time, Pallas kernels for 3%

profile of v5, /device:TPU:4, one launch (start us, length us, event | category | flops | bytes accessed | tf_op | source)
XLA Modules:
  0.0 147.3 jit_solution(16132860699793338993)
XLA Ops:
  0.7 0.0 copy-start.3
  0.7 1.3 pad_maximum_fusion.xg_ref
  2.0 0.0 copy-start
  2.0 1.6 %shard_map.86 = (bf16[2,48,1536]{2,1,0:T(8,128)(2,1)S(1)}, bf16[2,48,1536]{2,1,0:T(8,128)(2,1)S(1)}, bf16[2,48,1536]{2,1,0:T(8,128)(2,1)S(1)}, bf16[2,48,1536]{2...) custom-call(s32[8,48]{1,0:T(8,128)S(1)} %copy-done.5, ...), custom_call_target="tpu_custom_call" | custom-call | flops 301989888 | bytes 3147264 | tf_op jit(solution)/shard_map/pallas_call | solution.py:40
  3.7 3.8 %collective-permute-start = (bf16[2,48,1536]{2,1,0:T(8,128)(2,1)S(1)}, bf16[2,48,1536]{2,1,0:T(8,128)(2,1)S(1)}, u32[]{:S(2)}, u32[]{:S(2)}) collective-permute-start(bf16[2,48,1536]{2,1,0:T(8,128)(2,1)S(1)} %get-tuple-element.12), channel_id=1, source_target_pairs={{0,128},{64,192},{128,256},{192,320},{256,384},{320,448},{384,4},{... | collective-permute-start | bytes 884744 | tf_op jit(solution)/shard_map/ppermute | solution.py:247
  7.5 9.5 %collective-permute-start.1 = (bf16[2,48,1536]{2,1,0:T(8,128)(2,1)S(1)}, bf16[2,48,1536]{2,1,0:T(8,128)(2,1)S(1)}, u32[]{:S(2)}, u32[]{:S(2)}) collective-permute-start(bf16[2,48,1536]{2,1,0:T(8,128)(2,1)S(1)} %get-tuple-element.13), channel_id=1, source_target_pairs={{0,396},{64,460},{128,0},{192,64},{256,128},{320,192},{384,256},{4... | collective-permute-start | bytes 884744 | tf_op jit(solution)/shard_map/ppermute | solution.py:247
  17.0 1.9 %collective-permute-start.2 = (bf16[2,48,1536]{2,1,0:T(8,128)(2,1)S(1)}, bf16[2,48,1536]{2,1,0:T(8,128)(2,1)S(1)}, u32[]{:S(2)}, u32[]{:S(2)}) collective-permute-start(bf16[2,48,1536]{2,1,0:T(8,128)(2,1)S(1)} %get-tuple-element.14), channel_id=1, source_target_pairs={{0,192},{64,128},{128,320},{192,256},{256,448},{320,384},{384,68},... | collective-permute-start | bytes 884744 | tf_op jit(solution)/shard_map/ppermute | solution.py:247
  18.9 4.9 %collective-permute-start.3 = (bf16[2,48,1536]{2,1,0:T(8,128)(2,1)S(1)}, bf16[2,48,1536]{2,1,0:T(8,128)(2,1)S(1)}, u32[]{:S(2)}, u32[]{:S(2)}) collective-permute-start(bf16[2,48,1536]{2,1,0:T(8,128)(2,1)S(1)} %get-tuple-element.15), channel_id=1, source_target_pairs={{0,460},{64,396},{128,64},{192,0},{256,192},{320,128},{384,320},{4... | collective-permute-start | bytes 884744 | tf_op jit(solution)/shard_map/ppermute | solution.py:247
  23.8 1.9 %collective-permute-start.4 = (bf16[2,48,1536]{2,1,0:T(8,128)(2,1)}, bf16[2,48,1536]{2,1,0:T(8,128)(2,1)}, u32[]{:S(2)}, u32[]{:S(2)}) collective-permute-start(bf16[2,48,1536]{2,1,0:T(8,128)(2,1)} %get-tuple-element.16), channel_id=1, source_target_pairs={{0,256},{64,320},{128,384},{192,448},{256,4},{320,68},{384,132},{4... | collective-permute-start | bytes 884744 | tf_op jit(solution)/shard_map/ppermute | solution.py:247
  25.7 0.0 collective-permute-done.refs_2_
  25.7 4.9 %collective-permute-start.5 = (bf16[2,48,1536]{2,1,0:T(8,128)(2,1)S(1)}, bf16[2,48,1536]{2,1,0:T(8,128)(2,1)}, u32[]{:S(2)}, u32[]{:S(2)}) collective-permute-start(bf16[2,48,1536]{2,1,0:T(8,128)(2,1)S(1)} %get-tuple-element.17), channel_id=1, source_target_pairs={{0,332},{64,268},{128,460},{192,396},{256,64},{320,0},{384,192},{4... | collective-permute-start | bytes 884744 | tf_op jit(solution)/shard_map/ppermute | solution.py:247
  30.6 3.1 %all-gather = bf16[4,48,1536]{2,1,0:T(8,128)(2,1)S(1)} all-gather(bf16[2,48,1536]{2,1,0:T(8,128)(2,1)S(1)} %get-tuple-element.11), channel_id=2, replica_groups=mesh['zl'=4,'c'=2,'y'=4,'zh'=4,'x'=4] {'c'}, dimensions={0}, use_global_device_ids=true | all-gather | bytes 884736 | tf_op jit(solution)/shard_map/all_gather | solution.py:248
  33.7 0.0 collective-permute-done.2.refs_4_
  33.8 1.5 %shard_map.87 = bf16[288,1152]{1,0:T(8,128)(2,1)S(1)} custom-call(bf16[2,48,1536]{2,1,0:T(8,128)(2,1)S(1)} %get-tuple-element.10.refs_0_, bf16[2,2,48,1536]{3,2,1,0:T(8,128)(2,1)S(1)} %bitcast.19, bf16[2,48,1536]{2,1,0:T(8,128)(2,1)S(1)} %collective-permute-done.refs_2_, bf16[2,48,1536]{2,1,0:T(8,128)(2,1)S(1)} %collective-permute-done.1.refs_3_, ...), custom_call_target="tpu_custom_call" | custom-call | flops 1019215872 | bytes 6266880 | tf_op jit(solution)/shard_map/pallas_call | solution.py:40
  35.3 0.8 copy-done.2
  36.2 4.8 %all-to-all-start = ((bf16[4,72,1152]{2,1,0:T(8,128)(2,1)}), bf16[4,72,1152]{2,1,0:T(8,128)(2,1)S(1)}, u32[]{:S(2)}, u32[]{:S(2)}) async-start(bf16[4,72,1152]{2,1,0:T(8,128)(2,1)} %bitcast.18), calls=%async_computation | async-start | bytes 1327104 | tf_op jit(solution)/shard_map/all_to_all | solution.py:216
  41.0 1.1 collective-permute-done.5.refs_1_
  42.0 1.3 copy-done.4
  43.3 2.2 %shard_map.88.a_ref = bf16[96,1152]{1,0:T(8,128)(2,1)S(1)} custom-call(bf16[2,48,1536]{2,1,0:T(8,128)(2,1)} %collective-permute-done.4.refs_0_, bf16[2,48,1536]{2,1,0:T(8,128)(2,1)} %collective-permute-done.5.refs_1_, bf16[384,1536]{1,0:T(8,128)(2,1)S(1)} %bitcast.11, bf16[384,1536]{1,0:T(8,128)(2,1)S(1)} %bitcast.14, bf16[384,1536]{1,0:T(8,128)(2,1)S(1)} %bitcast.22), custom_call_target="tpu_custom_call" | custom-call | flops 3397386240 | bytes 4349952 | tf_op jit(solution)/shard_map/pallas_call | solution.py:40
  45.5 4.0 %all-to-all-done._.refs_0_ = bf16[4,72,1152]{2,1,0:T(8,128)(2,1)S(1)} async-done(((bf16[4,72,1152]{2,1,0:T(8,128)(2,1)}), bf16[4,72,1152]{2,1,0:T(8,128)(2,1)S(1)}, u32[]{:S(2)}, u32[]{:S(2)}) %all-to-all-start) | async-done | bytes 663584 | tf_op jit(solution)/shard_map/all_to_all | solution.py:216
  49.5 9.2 %all_to_all.20.refs_1_ = bf16[4,24,1152]{2,1,0:T(8,128)(2,1)S(1)} all-to-all(bf16[4,24,1152]{2,1,0:T(8,128)(2,1)S(1)} %bitcast.23), channel_id=1, replica_groups=mesh['zl'=4,'c'=2,'y'=4,'zh'=4,'x'=4] {'x'}, dimensions={0} | all-to-all | bytes 442368 | tf_op jit(solution)/shard_map/all_to_all | solution.py:216
  58.7 0.2 shard_map.90
  59.0 13.8 %all_gather.23.d_ref = bf16[384,896]{1,0:T(8,128)(2,1)S(1)} all-gather(bf16[96,896]{1,0:T(8,128)(2,1)S(1)} %shard_map.90), channel_id=1, replica_groups=mesh['zl'=4,'c'=2,'y'=4,'zh'=4,'x'=4] {'x'}, dimensions={0}, use_global_device_ids=true | all-gather | bytes 860160 | tf_op jit(solution)/shard_map/all_gather | solution.py:268
  72.7 1.8 %shard_map.91 = bf16[4,400,384]{2,1,0:T(8,128)(2,1)S(1)} custom-call(bf16[384,896]{1,0:T(8,128)(2,1)S(1)} %all_gather.23.d_ref, bf16[384,1536]{1,0:T(8,128)(2,1)S(1)} %bitcast.12, bf16[384,1536]{1,0:T(8,128)(2,1)S(1)} %bitcast.15), custom_call_target="tpu_custom_call" | custom-call | flops 905969664 | bytes 4276224 | tf_op jit(solution)/shard_map/pallas_call | solution.py:40
  74.6 18.2 %all_to_all.21.part_ref = bf16[4,400,384]{2,1,0:T(8,128)(2,1)S(1)} all-to-all(bf16[4,400,384]{2,1,0:T(8,128)(2,1)S(1)} %shard_map.91), channel_id=1, replica_groups=mesh['zl'=4,'c'=2,'y'=4,'zh'=4,'x'=4] {'y'}, dimensions={0} | all-to-all | bytes 2457600 | tf_op jit(solution)/shard_map/all_to_all | solution.py:216
  92.8 0.2 shard_map.92
  93.0 13.9 %all_to_all.22.back_ref = bf16[8,56,384]{2,1,0:T(8,128)(2,1)S(1)} all-to-all(bf16[8,56,384]{2,1,0:T(8,128)(2,1)S(1)} %shard_map.92), channel_id=1, replica_groups=mesh['zl'=4,'c'=2,'y'=4,'zh'=4,'x'=4] {'zl','c'}, dimensions={0} | all-to-all | bytes 688128 | tf_op jit(solution)/shard_map/all_to_all | solution.py:216
  106.8 0.4 shard_map.93
  107.2 26.3 %all-gather.1 = bf16[576,384]{1,0:T(8,128)(2,1)S(1)} all-gather(bf16[144,384]{1,0:T(8,128)(2,1)S(1)} %shard_map.93), channel_id=3, replica_groups=mesh['zl'=4,'c'=2,'y'=4,'zh'=4,'x'=4] {'zh'}, dimensions={0}, use_global_device_ids=true | all-gather | bytes 552960 | tf_op jit(solution)/shard_map/all_gather | solution.py:286
  133.5 0.1 shard_map.94
  133.6 12.9 %all-gather.2 = bf16[512,384]{1,0:T(8,128)(2,1)S(1)} all-gather(bf16[128,384]{1,0:T(8,128)(2,1)S(1)} %shard_map.94), channel_id=4, replica_groups=mesh['zl'=4,'c'=2,'y'=4,'zh'=4,'x'=4] {'y'}, dimensions={0}, use_global_device_ids=true | all-gather | bytes 491520 | tf_op jit(solution)/shard_map/all_gather | solution.py:291
  146.5 0.8 shard_map.95
  (14 shorter events, 0.0 us)
Async XLA Ops:
  0.6 1.4 copy-start.5
  0.6 33.1 %copy-start.1 = (bf16[1,384,1536]{2,1,0:T(8,128)(2,1)S(1)}, bf16[1,384,1536]{2,1,0:T(8,128)(2,1)}, u32[]{:S(2)}) copy-start(bf16[1,384,1536]{2,1,0:T(8,128)(2,1)} %param.12) | copy-start | bytes 3538948
  0.7 33.1 %copy-start.3 = (bf16[1,384,1536]{2,1,0:T(8,128)(2,1)S(1)}, bf16[1,384,1536]{2,1,0:T(8,128)(2,1)}, u32[]{:S(2)}) copy-start(bf16[1,384,1536]{2,1,0:T(8,128)(2,1)} %param.13) | copy-start | bytes 3538948
  2.0 31.8 %copy-start = (bf16[1,384,1536]{2,1,0:T(8,128)(2,1)S(1)}, bf16[1,384,1536]{2,1,0:T(8,128)(2,1)}, u32[]{:S(2)}) copy-start(bf16[1,384,1536]{2,1,0:T(8,128)(2,1)} %param.11) | copy-start | bytes 3538948
  3.7 22.0 %collective-permute-start = (bf16[2,48,1536]{2,1,0:T(8,128)(2,1)S(1)}, bf16[2,48,1536]{2,1,0:T(8,128)(2,1)S(1)}, u32[]{:S(2)}, u32[]{:S(2)}) collective-permute-start(bf16[2,48,1536]{2,1,0:T(8,128)(2,1)S(1)} %get-tuple-element.12), channel_id=1, source_target_pairs={{0,128},{64,192},{128,256},{192,320},{256,384},{320,448},{384,4},{... | collective-permute-start | bytes 884744 | tf_op jit(solution)/shard_map/ppermute | solution.py:247
  7.5 26.2 %collective-permute-start.1 = (bf16[2,48,1536]{2,1,0:T(8,128)(2,1)S(1)}, bf16[2,48,1536]{2,1,0:T(8,128)(2,1)S(1)}, u32[]{:S(2)}, u32[]{:S(2)}) collective-permute-start(bf16[2,48,1536]{2,1,0:T(8,128)(2,1)S(1)} %get-tuple-element.13), channel_id=1, source_target_pairs={{0,396},{64,460},{128,0},{192,64},{256,128},{320,192},{384,256},{4... | collective-permute-start | bytes 884744 | tf_op jit(solution)/shard_map/ppermute | solution.py:247
  17.0 16.7 %collective-permute-start.2 = (bf16[2,48,1536]{2,1,0:T(8,128)(2,1)S(1)}, bf16[2,48,1536]{2,1,0:T(8,128)(2,1)S(1)}, u32[]{:S(2)}, u32[]{:S(2)}) collective-permute-start(bf16[2,48,1536]{2,1,0:T(8,128)(2,1)S(1)} %get-tuple-element.14), channel_id=1, source_target_pairs={{0,192},{64,128},{128,320},{192,256},{256,448},{320,384},{384,68},... | collective-permute-start | bytes 884744 | tf_op jit(solution)/shard_map/ppermute | solution.py:247
  18.9 14.8 %collective-permute-start.3 = (bf16[2,48,1536]{2,1,0:T(8,128)(2,1)S(1)}, bf16[2,48,1536]{2,1,0:T(8,128)(2,1)S(1)}, u32[]{:S(2)}, u32[]{:S(2)}) collective-permute-start(bf16[2,48,1536]{2,1,0:T(8,128)(2,1)S(1)} %get-tuple-element.15), channel_id=1, source_target_pairs={{0,460},{64,396},{128,64},{192,0},{256,192},{320,128},{384,320},{4... | collective-permute-start | bytes 884744 | tf_op jit(solution)/shard_map/ppermute | solution.py:247
  23.8 17.2 %collective-permute-start.4 = (bf16[2,48,1536]{2,1,0:T(8,128)(2,1)}, bf16[2,48,1536]{2,1,0:T(8,128)(2,1)}, u32[]{:S(2)}, u32[]{:S(2)}) collective-permute-start(bf16[2,48,1536]{2,1,0:T(8,128)(2,1)} %get-tuple-element.16), channel_id=1, source_target_pairs={{0,256},{64,320},{128,384},{192,448},{256,4},{320,68},{384,132},{4... | collective-permute-start | bytes 884744 | tf_op jit(solution)/shard_map/ppermute | solution.py:247
  25.7 16.3 %collective-permute-start.5 = (bf16[2,48,1536]{2,1,0:T(8,128)(2,1)S(1)}, bf16[2,48,1536]{2,1,0:T(8,128)(2,1)}, u32[]{:S(2)}, u32[]{:S(2)}) collective-permute-start(bf16[2,48,1536]{2,1,0:T(8,128)(2,1)S(1)} %get-tuple-element.17), channel_id=1, source_target_pairs={{0,332},{64,268},{128,460},{192,396},{256,64},{320,0},{384,192},{4... | collective-permute-start | bytes 884744 | tf_op jit(solution)/shard_map/ppermute | solution.py:247
  35.3 0.9 copy-start.2
  36.2 13.3 %all-to-all-start = ((bf16[4,72,1152]{2,1,0:T(8,128)(2,1)}), bf16[4,72,1152]{2,1,0:T(8,128)(2,1)S(1)}, u32[]{:S(2)}, u32[]{:S(2)}) async-start(bf16[4,72,1152]{2,1,0:T(8,128)(2,1)} %bitcast.18), calls=%async_computation | async-start | bytes 1327104 | tf_op jit(solution)/shard_map/all_to_all | solution.py:216
  42.0 1.3 copy-start.4
  92.8 14.1 %copy-start.6 = (bf16[8,48]{1,0:T(8,128)(2,1)S(1)}, bf16[8,48]{1,0:T(8,128)(2,1)}, u32[]{:S(2)}) copy-start(bf16[8,48]{1,0:T(8,128)(2,1)} %weights_ref.1) | copy-start | bytes 2308

commit v6 on v5

--- a/solution.py
+++ b/solution.py
@@ -133,20 +133,21 @@
     pick = (iota((PAD, LANES), 0) == iota((PAD, LANES), 1)).astype(BF16)
     lines = dot(pick, d_scores, 1, 1)
     line = iota((PAD, rows), 0)
-    block = in_blocks(iota((PAD, rows), 1), rows) // each
+    block = in_blocks(iota((1, rows), 1), rows) // each
     apart = jnp.where(line == block, lines[0:1, :], jnp.where(line == block + shards, lines[1:2, :], 0.0))
-    lane = in_blocks(iota((rows, LANES), 0), rows) % each
+    lane = in_blocks(iota((rows, 1), 0), rows) % each
     return dot(apart.astype(BF16), (iota((rows, LANES), 1) == lane).astype(BF16), 1, 0)
 
 
-def backward_kernel(shards, d_ref, gate_ref, up_ref, out_ref):
+def backward_kernel(shards, d_ref, gate_ref, up_ref, out_ref, w_ref):
     rows, hidden = d_ref.shape[0], gate_ref.shape[0]
     parts, _, share = out_ref.shape
     block = score_block(d_ref[:, 2 * hidden :], shards).astype(BF16)
     for k in range(parts):
         cols = slice(k * share, (k + 1) * share)
-        total = dot(d_ref[:, :hidden], gate_ref[:, cols], 1, 0)
-        total += dot(d_ref[:, hidden : 2 * hidden], up_ref[:, cols], 1, 0)
+        w_ref[k % 2, :hidden, :] = gate_ref[:, cols]
+        w_ref[k % 2, hidden:, :] = up_ref[:, cols]
+        total = dot(d_ref[:, : 2 * hidden], w_ref[k % 2], 1, 0)
         out_ref[k, :rows, :] = total.astype(BF16)
         out_ref[k, rows:, :] = jnp.zeros((PAD, share), BF16)
         out_ref[k, rows:, :LANES] = block
@@ -238,7 +239,7 @@
     sent = call(
         pick_kernel,
         [sds((2, taken, width))] * experts,
-        (picks, jnp.stack([layer_input, out_grad])),
+        (picks, jnp.concatenate([layer_input, out_grad]).reshape(2, tokens, width)),
         flops=4 * rows * tokens * width,
         scratch=[pltpu.VMEM((rows, tokens), BF16)],
     )
@@ -271,6 +272,7 @@
         sds((ny, rows + PAD, share)),
         (d, w_gate, w_up),
         flops=4 * rows * hidden * width,
+        scratch=[pltpu.VMEM((2, 2 * hidden, share), BF16)],
     )
     summed = call(
         sum_kernel,

time: 148 us -> 148 us (level)
  no operation moved by 1% of the time
where the time goes in v6:
time: 148 us; the launch traced here: 147 us
  blocking collectives  97.4 us (66%)
  starting transfers between devices  31.7 us (21%)
  Pallas kernels  8.67 us (6%)
  waiting for transfers between devices  5.08 us (3%)
  local copies, waits for them, and re-layouts  2.14 us (1%)
    all_to_all x3, blocking collectives, exchange(): return lax.all_to_all(a, axes, split_axis=0, concat_axis=0, tiled=True)  41.3 us
    ppermute x6, starting transfers between devices, local(): got[i] = lax.ppermute(sent[i], RING, along_z(*BLOCKS[i]))  26.9 us
    all_gather x1, blocking collectives, local(): over_zh = lax.all_gather(mine, 'zh')  26.4 us
    all_gather x1, blocking collectives, local(): d = lax.all_gather(d_block, 'x', tiled=True)  13.8 us
    all_gather x1, blocking collectives, local(): lax.all_gather(token_grad, 'y')  12.9 us
    pallas_call x10, Pallas kernels, call(): pl.pallas_call(kernel, out_shape=outs, in_specs=specs or [VMEM] * len(arg...  8.67 us
    all_to_all x1, starting transfers between devices, exchange(): return lax.all_to_all(a, axes, split_axis=0, concat_axis=0, tiled=True)  4.81 us
    all_to_all x1, waiting for transfers between devices, exchange(): return lax.all_to_all(a, axes, split_axis=0, concat_axis=0, tiled=True)  4.03 us
  transfers between devices with their start and end apart: 7, of which 2 were waited for; matrix products, arithmetic and copies ran while one was open for 0% of the time, Pallas kernels for 3%

profile of v6, /device:TPU:4, one launch (start us, length us, event | category | flops | bytes accessed | tf_op | source)
XLA Modules:
  0.0 147.2 jit_solution(12676484194637165584)
XLA Ops:
  0.7 0.0 copy-start.3
  0.7 1.3 pad_maximum_fusion
  2.0 0.0 copy-start
  2.0 1.6 %shard_map.86 = (bf16[2,48,1536]{2,1,0:T(8,128)(2,1)S(1)}, bf16[2,48,1536]{2,1,0:T(8,128)(2,1)S(1)}, bf16[2,48,1536]{2,1,0:T(8,128)(2,1)S(1)}, bf16[2,48,1536]{2...) custom-call(s32[8,48]{1,0:T(8,128)S(1)} %copy-done.5, ...), custom_call_target="tpu_custom_call" | custom-call | flops 301989888 | bytes 3147264 | tf_op jit(solution)/shard_map/pallas_call | solution.py:40
  3.7 3.8 %collective-permute-start = (bf16[2,48,1536]{2,1,0:T(8,128)(2,1)S(1)}, bf16[2,48,1536]{2,1,0:T(8,128)(2,1)S(1)}, u32[]{:S(2)}, u32[]{:S(2)}) collective-permute-start(bf16[2,48,1536]{2,1,0:T(8,128)(2,1)S(1)} %get-tuple-element.12), channel_id=1, source_target_pairs={{0,128},{64,192},{128,256},{192,320},{256,384},{320,448},{384,4},{... | collective-permute-start | bytes 884744 | tf_op jit(solution)/shard_map/ppermute | solution.py:248
  7.5 9.5 %collective-permute-start.1 = (bf16[2,48,1536]{2,1,0:T(8,128)(2,1)S(1)}, bf16[2,48,1536]{2,1,0:T(8,128)(2,1)S(1)}, u32[]{:S(2)}, u32[]{:S(2)}) collective-permute-start(bf16[2,48,1536]{2,1,0:T(8,128)(2,1)S(1)} %get-tuple-element.13), channel_id=1, source_target_pairs={{0,396},{64,460},{128,0},{192,64},{256,128},{320,192},{384,256},{4... | collective-permute-start | bytes 884744 | tf_op jit(solution)/shard_map/ppermute | solution.py:248
  17.0 1.9 %collective-permute-start.2 = (bf16[2,48,1536]{2,1,0:T(8,128)(2,1)S(1)}, bf16[2,48,1536]{2,1,0:T(8,128)(2,1)S(1)}, u32[]{:S(2)}, u32[]{:S(2)}) collective-permute-start(bf16[2,48,1536]{2,1,0:T(8,128)(2,1)S(1)} %get-tuple-element.14), channel_id=1, source_target_pairs={{0,192},{64,128},{128,320},{192,256},{256,448},{320,384},{384,68},... | collective-permute-start | bytes 884744 | tf_op jit(solution)/shard_map/ppermute | solution.py:248
  18.9 4.9 %collective-permute-start.3 = (bf16[2,48,1536]{2,1,0:T(8,128)(2,1)S(1)}, bf16[2,48,1536]{2,1,0:T(8,128)(2,1)S(1)}, u32[]{:S(2)}, u32[]{:S(2)}) collective-permute-start(bf16[2,48,1536]{2,1,0:T(8,128)(2,1)S(1)} %get-tuple-element.15), channel_id=1, source_target_pairs={{0,460},{64,396},{128,64},{192,0},{256,192},{320,128},{384,320},{4... | collective-permute-start | bytes 884744 | tf_op jit(solution)/shard_map/ppermute | solution.py:248
  23.8 1.9 %collective-permute-start.4 = (bf16[2,48,1536]{2,1,0:T(8,128)(2,1)}, bf16[2,48,1536]{2,1,0:T(8,128)(2,1)}, u32[]{:S(2)}, u32[]{:S(2)}) collective-permute-start(bf16[2,48,1536]{2,1,0:T(8,128)(2,1)} %get-tuple-element.16), channel_id=1, source_target_pairs={{0,256},{64,320},{128,384},{192,448},{256,4},{320,68},{384,132},{4... | collective-permute-start | bytes 884744 | tf_op jit(solution)/shard_map/ppermute | solution.py:248
  25.7 0.0 collective-permute-done.refs_2_
  25.7 4.9 %collective-permute-start.5 = (bf16[2,48,1536]{2,1,0:T(8,128)(2,1)S(1)}, bf16[2,48,1536]{2,1,0:T(8,128)(2,1)}, u32[]{:S(2)}, u32[]{:S(2)}) collective-permute-start(bf16[2,48,1536]{2,1,0:T(8,128)(2,1)S(1)} %get-tuple-element.17), channel_id=1, source_target_pairs={{0,332},{64,268},{128,460},{192,396},{256,64},{320,0},{384,192},{4... | collective-permute-start | bytes 884744 | tf_op jit(solution)/shard_map/ppermute | solution.py:248
  30.6 3.1 %all-gather = bf16[4,48,1536]{2,1,0:T(8,128)(2,1)S(1)} all-gather(bf16[2,48,1536]{2,1,0:T(8,128)(2,1)S(1)} %get-tuple-element.11), channel_id=2, replica_groups=mesh['zl'=4,'c'=2,'y'=4,'zh'=4,'x'=4] {'c'}, dimensions={0}, use_global_device_ids=true | all-gather | bytes 884736 | tf_op jit(solution)/shard_map/all_gather | solution.py:249
  33.7 0.0 collective-permute-done.3.refs_5_
  33.8 1.5 %shard_map.87 = bf16[288,1152]{1,0:T(8,128)(2,1)S(1)} custom-call(bf16[2,48,1536]{2,1,0:T(8,128)(2,1)S(1)} %get-tuple-element.10.refs_0_, bf16[2,2,48,1536]{3,2,1,0:T(8,128)(2,1)S(1)} %bitcast.18, bf16[2,48,1536]{2,1,0:T(8,128)(2,1)S(1)} %collective-permute-done.refs_2_, bf16[2,48,1536]{2,1,0:T(8,128)(2,1)S(1)} %collective-permute-done.1.refs_3_, ...), custom_call_target="tpu_custom_call" | custom-call | flops 1019215872 | bytes 6266880 | tf_op jit(solution)/shard_map/pallas_call | solution.py:40
  35.3 0.8 copy-done.2
  36.2 4.8 %all-to-all-start = ((bf16[4,72,1152]{2,1,0:T(8,128)(2,1)}), bf16[4,72,1152]{2,1,0:T(8,128)(2,1)S(1)}, u32[]{:S(2)}, u32[]{:S(2)}) async-start(bf16[4,72,1152]{2,1,0:T(8,128)(2,1)} %bitcast.17), calls=%async_computation | async-start | bytes 1327104 | tf_op jit(solution)/shard_map/all_to_all | solution.py:217
  41.0 1.0 collective-permute-done.5.refs_1_
  42.0 1.3 copy-done.4
  43.3 2.2 %shard_map.88.a_ref = bf16[96,1152]{1,0:T(8,128)(2,1)S(1)} custom-call(bf16[2,48,1536]{2,1,0:T(8,128)(2,1)} %collective-permute-done.4.refs_0_, bf16[2,48,1536]{2,1,0:T(8,128)(2,1)} %collective-permute-done.5.refs_1_, bf16[384,1536]{1,0:T(8,128)(2,1)S(1)} %bitcast.10, bf16[384,1536]{1,0:T(8,128)(2,1)S(1)} %bitcast.13, bf16[384,1536]{1,0:T(8,128)(2,1)S(1)} %bitcast.21), custom_call_target="tpu_custom_call" | custom-call | flops 3397386240 | bytes 4349952 | tf_op jit(solution)/shard_map/pallas_call | solution.py:40
  45.5 4.0 %all-to-all-done._.refs_0_ = bf16[4,72,1152]{2,1,0:T(8,128)(2,1)S(1)} async-done(((bf16[4,72,1152]{2,1,0:T(8,128)(2,1)}), bf16[4,72,1152]{2,1,0:T(8,128)(2,1)S(1)}, u32[]{:S(2)}, u32[]{:S(2)}) %all-to-all-start) | async-done | bytes 663584 | tf_op jit(solution)/shard_map/all_to_all | solution.py:217
  49.5 9.2 %all_to_all.20.refs_1_ = bf16[4,24,1152]{2,1,0:T(8,128)(2,1)S(1)} all-to-all(bf16[4,24,1152]{2,1,0:T(8,128)(2,1)S(1)} %bitcast.22), channel_id=1, replica_groups=mesh['zl'=4,'c'=2,'y'=4,'zh'=4,'x'=4] {'x'}, dimensions={0} | all-to-all | bytes 442368 | tf_op jit(solution)/shard_map/all_to_all | solution.py:217
  58.7 0.2 shard_map.90
  59.0 13.8 %all_gather.23.d_ref = bf16[384,896]{1,0:T(8,128)(2,1)S(1)} all-gather(bf16[96,896]{1,0:T(8,128)(2,1)S(1)} %shard_map.90), channel_id=1, replica_groups=mesh['zl'=4,'c'=2,'y'=4,'zh'=4,'x'=4] {'x'}, dimensions={0}, use_global_device_ids=true | all-gather | bytes 860160 | tf_op jit(solution)/shard_map/all_gather | solution.py:269
  72.7 1.7 %shard_map.91 = bf16[4,400,384]{2,1,0:T(8,128)(2,1)S(1)} custom-call(bf16[384,896]{1,0:T(8,128)(2,1)S(1)} %all_gather.23.d_ref, bf16[384,1536]{1,0:T(8,128)(2,1)S(1)} %bitcast.11, bf16[384,1536]{1,0:T(8,128)(2,1)S(1)} %bitcast.14), custom_call_target="tpu_custom_call" | custom-call | flops 905969664 | bytes 4276224 | tf_op jit(solution)/shard_map/pallas_call | solution.py:40
  74.4 18.2 %all_to_all.21.part_ref = bf16[4,400,384]{2,1,0:T(8,128)(2,1)S(1)} all-to-all(bf16[4,400,384]{2,1,0:T(8,128)(2,1)S(1)} %shard_map.91), channel_id=1, replica_groups=mesh['zl'=4,'c'=2,'y'=4,'zh'=4,'x'=4] {'y'}, dimensions={0} | all-to-all | bytes 2457600 | tf_op jit(solution)/shard_map/all_to_all | solution.py:217
  92.6 0.2 shard_map.92
  92.8 13.9 %all_to_all.22.back_ref = bf16[8,56,384]{2,1,0:T(8,128)(2,1)S(1)} all-to-all(bf16[8,56,384]{2,1,0:T(8,128)(2,1)S(1)} %shard_map.92), channel_id=1, replica_groups=mesh['zl'=4,'c'=2,'y'=4,'zh'=4,'x'=4] {'zl','c'}, dimensions={0} | all-to-all | bytes 688128 | tf_op jit(solution)/shard_map/all_to_all | solution.py:217
  106.7 0.3 shard_map.93
  107.0 26.4 %all-gather.1 = bf16[576,384]{1,0:T(8,128)(2,1)S(1)} all-gather(bf16[144,384]{1,0:T(8,128)(2,1)S(1)} %shard_map.93), channel_id=3, replica_groups=mesh['zl'=4,'c'=2,'y'=4,'zh'=4,'x'=4] {'zh'}, dimensions={0}, use_global_device_ids=true | all-gather | bytes 552960 | tf_op jit(solution)/shard_map/all_gather | solution.py:288
  133.4 0.1 shard_map.94
  133.5 12.9 %all-gather.2 = bf16[512,384]{1,0:T(8,128)(2,1)S(1)} all-gather(bf16[128,384]{1,0:T(8,128)(2,1)S(1)} %shard_map.94), channel_id=4, replica_groups=mesh['zl'=4,'c'=2,'y'=4,'zh'=4,'x'=4] {'y'}, dimensions={0}, use_global_device_ids=true | all-gather | bytes 491520 | tf_op jit(solution)/shard_map/all_gather | solution.py:293
  146.4 0.8 shard_map.95
  (14 shorter events, 0.0 us)
Async XLA Ops:
  0.6 1.4 copy-start.5
  0.6 33.1 %copy-start.1 = (bf16[1,384,1536]{2,1,0:T(8,128)(2,1)S(1)}, bf16[1,384,1536]{2,1,0:T(8,128)(2,1)}, u32[]{:S(2)}) copy-start(bf16[1,384,1536]{2,1,0:T(8,128)(2,1)} %param.12) | copy-start | bytes 3538948
  0.7 33.1 %copy-start.3 = (bf16[1,384,1536]{2,1,0:T(8,128)(2,1)S(1)}, bf16[1,384,1536]{2,1,0:T(8,128)(2,1)}, u32[]{:S(2)}) copy-start(bf16[1,384,1536]{2,1,0:T(8,128)(2,1)} %param.13) | copy-start | bytes 3538948
  2.0 31.8 %copy-start = (bf16[1,384,1536]{2,1,0:T(8,128)(2,1)S(1)}, bf16[1,384,1536]{2,1,0:T(8,128)(2,1)}, u32[]{:S(2)}) copy-start(bf16[1,384,1536]{2,1,0:T(8,128)(2,1)} %param.11) | copy-start | bytes 3538948
  3.7 22.1 %collective-permute-start = (bf16[2,48,1536]{2,1,0:T(8,128)(2,1)S(1)}, bf16[2,48,1536]{2,1,0:T(8,128)(2,1)S(1)}, u32[]{:S(2)}, u32[]{:S(2)}) collective-permute-start(bf16[2,48,1536]{2,1,0:T(8,128)(2,1)S(1)} %get-tuple-element.12), channel_id=1, source_target_pairs={{0,128},{64,192},{128,256},{192,320},{256,384},{320,448},{384,4},{... | collective-permute-start | bytes 884744 | tf_op jit(solution)/shard_map/ppermute | solution.py:248
  7.5 26.3 %collective-permute-start.1 = (bf16[2,48,1536]{2,1,0:T(8,128)(2,1)S(1)}, bf16[2,48,1536]{2,1,0:T(8,128)(2,1)S(1)}, u32[]{:S(2)}, u32[]{:S(2)}) collective-permute-start(bf16[2,48,1536]{2,1,0:T(8,128)(2,1)S(1)} %get-tuple-element.13), channel_id=1, source_target_pairs={{0,396},{64,460},{128,0},{192,64},{256,128},{320,192},{384,256},{4... | collective-permute-start | bytes 884744 | tf_op jit(solution)/shard_map/ppermute | solution.py:248
  17.0 16.7 %collective-permute-start.2 = (bf16[2,48,1536]{2,1,0:T(8,128)(2,1)S(1)}, bf16[2,48,1536]{2,1,0:T(8,128)(2,1)S(1)}, u32[]{:S(2)}, u32[]{:S(2)}) collective-permute-start(bf16[2,48,1536]{2,1,0:T(8,128)(2,1)S(1)} %get-tuple-element.14), channel_id=1, source_target_pairs={{0,192},{64,128},{128,320},{192,256},{256,448},{320,384},{384,68},... | collective-permute-start | bytes 884744 | tf_op jit(solution)/shard_map/ppermute | solution.py:248
  18.9 14.8 %collective-permute-start.3 = (bf16[2,48,1536]{2,1,0:T(8,128)(2,1)S(1)}, bf16[2,48,1536]{2,1,0:T(8,128)(2,1)S(1)}, u32[]{:S(2)}, u32[]{:S(2)}) collective-permute-start(bf16[2,48,1536]{2,1,0:T(8,128)(2,1)S(1)} %get-tuple-element.15), channel_id=1, source_target_pairs={{0,460},{64,396},{128,64},{192,0},{256,192},{320,128},{384,320},{4... | collective-permute-start | bytes 884744 | tf_op jit(solution)/shard_map/ppermute | solution.py:248
  23.8 17.2 %collective-permute-start.4 = (bf16[2,48,1536]{2,1,0:T(8,128)(2,1)}, bf16[2,48,1536]{2,1,0:T(8,128)(2,1)}, u32[]{:S(2)}, u32[]{:S(2)}) collective-permute-start(bf16[2,48,1536]{2,1,0:T(8,128)(2,1)} %get-tuple-element.16), channel_id=1, source_target_pairs={{0,256},{64,320},{128,384},{192,448},{256,4},{320,68},{384,132},{4... | collective-permute-start | bytes 884744 | tf_op jit(solution)/shard_map/ppermute | solution.py:248
  25.7 16.3 %collective-permute-start.5 = (bf16[2,48,1536]{2,1,0:T(8,128)(2,1)S(1)}, bf16[2,48,1536]{2,1,0:T(8,128)(2,1)}, u32[]{:S(2)}, u32[]{:S(2)}) collective-permute-start(bf16[2,48,1536]{2,1,0:T(8,128)(2,1)S(1)} %get-tuple-element.17), channel_id=1, source_target_pairs={{0,332},{64,268},{128,460},{192,396},{256,64},{320,0},{384,192},{4... | collective-permute-start | bytes 884744 | tf_op jit(solution)/shard_map/ppermute | solution.py:248
  35.3 0.9 copy-start.2
  36.2 13.3 %all-to-all-start = ((bf16[4,72,1152]{2,1,0:T(8,128)(2,1)}), bf16[4,72,1152]{2,1,0:T(8,128)(2,1)S(1)}, u32[]{:S(2)}, u32[]{:S(2)}) async-start(bf16[4,72,1152]{2,1,0:T(8,128)(2,1)} %bitcast.17), calls=%async_computation | async-start | bytes 1327104 | tf_op jit(solution)/shard_map/all_to_all | solution.py:217
  42.0 1.3 copy-start.4
  92.6 14.1 %copy-start.6 = (bf16[8,48]{1,0:T(8,128)(2,1)S(1)}, bf16[8,48]{1,0:T(8,128)(2,1)}, u32[]{:S(2)}) copy-start(bf16[8,48]{1,0:T(8,128)(2,1)} %weights_ref.1) | copy-start | bytes 2308

commit v7 on v6

--- a/solution.py
+++ b/solution.py
@@ -130,13 +130,13 @@
 def score_block(d_scores, shards):
     rows = d_scores.shape[0]
     each = rows // shards
-    pick = (iota((PAD, LANES), 0) == iota((PAD, LANES), 1)).astype(BF16)
-    lines = dot(pick, d_scores, 1, 1)
-    line = iota((PAD, rows), 0)
     block = in_blocks(iota((1, rows), 1), rows) // each
-    apart = jnp.where(line == block, lines[0:1, :], jnp.where(line == block + shards, lines[1:2, :], 0.0))
-    lane = in_blocks(iota((rows, 1), 0), rows) % each
-    return dot(apart.astype(BF16), (iota((rows, LANES), 1) == lane).astype(BF16), 1, 0)
+    own = (iota((PAD, rows), 0) == block).astype(BF16)
+    here = iota((rows, LANES), 1) == in_blocks(iota((rows, 1), 0), rows) % each
+    values = d_scores.astype(F32)
+    high, low = (jnp.where(here, values[:, i : i + 1], 0.0).astype(BF16) for i in range(2))
+    both = dot(own, jnp.concatenate([high, low], axis=1), 1, 0)
+    return jnp.concatenate([both[:shards, :LANES], both[:shards, LANES:]], axis=0)
 
 
 def backward_kernel(shards, d_ref, gate_ref, up_ref, out_ref, w_ref):

time: 148 us -> 148 us (level)
  no operation moved by 1% of the time
where the time goes in v7:
time: 148 us; the launch traced here: 147 us
  blocking collectives  97.4 us (66%)
  starting transfers between devices  31.7 us (21%)
  Pallas kernels  8.68 us (6%)
  waiting for transfers between devices  5.08 us (3%)
  local copies, waits for them, and re-layouts  2.14 us (1%)
    all_to_all x3, blocking collectives, exchange(): return lax.all_to_all(a, axes, split_axis=0, concat_axis=0, tiled=True)  41.3 us
    ppermute x6, starting transfers between devices, local(): got[i] = lax.ppermute(sent[i], RING, along_z(*BLOCKS[i]))  26.9 us
    all_gather x1, blocking collectives, local(): over_zh = lax.all_gather(mine, 'zh')  26.3 us
    all_gather x1, blocking collectives, local(): d = lax.all_gather(d_block, 'x', tiled=True)  13.8 us
    all_gather x1, blocking collectives, local(): lax.all_gather(token_grad, 'y')  12.9 us
    pallas_call x10, Pallas kernels, call(): pl.pallas_call(kernel, out_shape=outs, in_specs=specs or [VMEM] * len(arg...  8.68 us
    all_to_all x1, starting transfers between devices, exchange(): return lax.all_to_all(a, axes, split_axis=0, concat_axis=0, tiled=True)  4.81 us
    all_to_all x1, waiting for transfers between devices, exchange(): return lax.all_to_all(a, axes, split_axis=0, concat_axis=0, tiled=True)  4.03 us
  transfers between devices with their start and end apart: 7, of which 2 were waited for; matrix products, arithmetic and copies ran while one was open for 0% of the time, Pallas kernels for 3%

profile of v7, /device:TPU:4, one launch (start us, length us, event | category | flops | bytes accessed | tf_op | source)
XLA Modules:
  0.0 147.1 jit_solution(5245897292327439853)
XLA Ops:
  0.7 0.0 copy-start.3
  0.7 1.3 pad_maximum_fusion
  2.0 0.0 copy-start
  2.0 1.6 %shard_map.86 = (bf16[2,48,1536]{2,1,0:T(8,128)(2,1)S(1)}, bf16[2,48,1536]{2,1,0:T(8,128)(2,1)S(1)}, bf16[2,48,1536]{2,1,0:T(8,128)(2,1)S(1)}, bf16[2,48,1536]{2...) custom-call(s32[8,48]{1,0:T(8,128)S(1)} %copy-done.5, ...), custom_call_target="tpu_custom_call" | custom-call | flops 301989888 | bytes 3147264 | tf_op jit(solution)/shard_map/pallas_call | solution.py:40
  3.7 3.8 %collective-permute-start = (bf16[2,48,1536]{2,1,0:T(8,128)(2,1)S(1)}, bf16[2,48,1536]{2,1,0:T(8,128)(2,1)S(1)}, u32[]{:S(2)}, u32[]{:S(2)}) collective-permute-start(bf16[2,48,1536]{2,1,0:T(8,128)(2,1)S(1)} %get-tuple-element.12), channel_id=1, source_target_pairs={{0,128},{64,192},{128,256},{192,320},{256,384},{320,448},{384,4},{... | collective-permute-start | bytes 884744 | tf_op jit(solution)/shard_map/ppermute | solution.py:248
  7.5 9.5 %collective-permute-start.1 = (bf16[2,48,1536]{2,1,0:T(8,128)(2,1)S(1)}, bf16[2,48,1536]{2,1,0:T(8,128)(2,1)S(1)}, u32[]{:S(2)}, u32[]{:S(2)}) collective-permute-start(bf16[2,48,1536]{2,1,0:T(8,128)(2,1)S(1)} %get-tuple-element.13), channel_id=1, source_target_pairs={{0,396},{64,460},{128,0},{192,64},{256,128},{320,192},{384,256},{4... | collective-permute-start | bytes 884744 | tf_op jit(solution)/shard_map/ppermute | solution.py:248
  17.0 1.9 %collective-permute-start.2 = (bf16[2,48,1536]{2,1,0:T(8,128)(2,1)S(1)}, bf16[2,48,1536]{2,1,0:T(8,128)(2,1)S(1)}, u32[]{:S(2)}, u32[]{:S(2)}) collective-permute-start(bf16[2,48,1536]{2,1,0:T(8,128)(2,1)S(1)} %get-tuple-element.14), channel_id=1, source_target_pairs={{0,192},{64,128},{128,320},{192,256},{256,448},{320,384},{384,68},... | collective-permute-start | bytes 884744 | tf_op jit(solution)/shard_map/ppermute | solution.py:248
  18.9 4.9 %collective-permute-start.3 = (bf16[2,48,1536]{2,1,0:T(8,128)(2,1)S(1)}, bf16[2,48,1536]{2,1,0:T(8,128)(2,1)S(1)}, u32[]{:S(2)}, u32[]{:S(2)}) collective-permute-start(bf16[2,48,1536]{2,1,0:T(8,128)(2,1)S(1)} %get-tuple-element.15), channel_id=1, source_target_pairs={{0,460},{64,396},{128,64},{192,0},{256,192},{320,128},{384,320},{4... | collective-permute-start | bytes 884744 | tf_op jit(solution)/shard_map/ppermute | solution.py:248
  23.8 1.9 %collective-permute-start.4 = (bf16[2,48,1536]{2,1,0:T(8,128)(2,1)}, bf16[2,48,1536]{2,1,0:T(8,128)(2,1)}, u32[]{:S(2)}, u32[]{:S(2)}) collective-permute-start(bf16[2,48,1536]{2,1,0:T(8,128)(2,1)} %get-tuple-element.16), channel_id=1, source_target_pairs={{0,256},{64,320},{128,384},{192,448},{256,4},{320,68},{384,132},{4... | collective-permute-start | bytes 884744 | tf_op jit(solution)/shard_map/ppermute | solution.py:248
  25.7 0.0 collective-permute-done.refs_2_
  25.7 4.9 %collective-permute-start.5 = (bf16[2,48,1536]{2,1,0:T(8,128)(2,1)S(1)}, bf16[2,48,1536]{2,1,0:T(8,128)(2,1)}, u32[]{:S(2)}, u32[]{:S(2)}) collective-permute-start(bf16[2,48,1536]{2,1,0:T(8,128)(2,1)S(1)} %get-tuple-element.17), channel_id=1, source_target_pairs={{0,332},{64,268},{128,460},{192,396},{256,64},{320,0},{384,192},{4... | collective-permute-start | bytes 884744 | tf_op jit(solution)/shard_map/ppermute | solution.py:248
  30.6 3.1 %all-gather = bf16[4,48,1536]{2,1,0:T(8,128)(2,1)S(1)} all-gather(bf16[2,48,1536]{2,1,0:T(8,128)(2,1)S(1)} %get-tuple-element.11), channel_id=2, replica_groups=mesh['zl'=4,'c'=2,'y'=4,'zh'=4,'x'=4] {'c'}, dimensions={0}, use_global_device_ids=true | all-gather | bytes 884736 | tf_op jit(solution)/shard_map/all_gather | solution.py:249
  33.7 0.0 collective-permute-done.3.refs_5_
  33.8 1.5 %shard_map.87 = bf16[288,1152]{1,0:T(8,128)(2,1)S(1)} custom-call(bf16[2,48,1536]{2,1,0:T(8,128)(2,1)S(1)} %get-tuple-element.10.refs_0_, bf16[2,2,48,1536]{3,2,1,0:T(8,128)(2,1)S(1)} %bitcast.18, bf16[2,48,1536]{2,1,0:T(8,128)(2,1)S(1)} %collective-permute-done.refs_2_, bf16[2,48,1536]{2,1,0:T(8,128)(2,1)S(1)} %collective-permute-done.1.refs_3_, ...), custom_call_target="tpu_custom_call" | custom-call | flops 1019215872 | bytes 6266880 | tf_op jit(solution)/shard_map/pallas_call | solution.py:40
  35.3 0.8 copy-done.2
  36.2 4.8 %all-to-all-start = ((bf16[4,72,1152]{2,1,0:T(8,128)(2,1)}), bf16[4,72,1152]{2,1,0:T(8,128)(2,1)S(1)}, u32[]{:S(2)}, u32[]{:S(2)}) async-start(bf16[4,72,1152]{2,1,0:T(8,128)(2,1)} %bitcast.17), calls=%async_computation | async-start | bytes 1327104 | tf_op jit(solution)/shard_map/all_to_all | solution.py:217
  41.0 1.0 collective-permute-done.5.refs_1_
  42.0 1.3 copy-done.4
  43.3 2.2 %shard_map.88.a_ref = bf16[96,1152]{1,0:T(8,128)(2,1)S(1)} custom-call(bf16[2,48,1536]{2,1,0:T(8,128)(2,1)} %collective-permute-done.4.refs_0_, bf16[2,48,1536]{2,1,0:T(8,128)(2,1)} %collective-permute-done.5.refs_1_, bf16[384,1536]{1,0:T(8,128)(2,1)S(1)} %bitcast.10, bf16[384,1536]{1,0:T(8,128)(2,1)S(1)} %bitcast.13, bf16[384,1536]{1,0:T(8,128)(2,1)S(1)} %bitcast.21), custom_call_target="tpu_custom_call" | custom-call | flops 3397386240 | bytes 4349952 | tf_op jit(solution)/shard_map/pallas_call | solution.py:40
  45.5 4.0 %all-to-all-done._.refs_0_ = bf16[4,72,1152]{2,1,0:T(8,128)(2,1)S(1)} async-done(((bf16[4,72,1152]{2,1,0:T(8,128)(2,1)}), bf16[4,72,1152]{2,1,0:T(8,128)(2,1)S(1)}, u32[]{:S(2)}, u32[]{:S(2)}) %all-to-all-start) | async-done | bytes 663584 | tf_op jit(solution)/shard_map/all_to_all | solution.py:217
  49.5 9.2 %all_to_all.20.refs_1_ = bf16[4,24,1152]{2,1,0:T(8,128)(2,1)S(1)} all-to-all(bf16[4,24,1152]{2,1,0:T(8,128)(2,1)S(1)} %bitcast.22), channel_id=1, replica_groups=mesh['zl'=4,'c'=2,'y'=4,'zh'=4,'x'=4] {'x'}, dimensions={0} | all-to-all | bytes 442368 | tf_op jit(solution)/shard_map/all_to_all | solution.py:217
  58.7 0.2 shard_map.90
  59.0 13.8 %all_gather.23.d_ref = bf16[384,896]{1,0:T(8,128)(2,1)S(1)} all-gather(bf16[96,896]{1,0:T(8,128)(2,1)S(1)} %shard_map.90), channel_id=1, replica_groups=mesh['zl'=4,'c'=2,'y'=4,'zh'=4,'x'=4] {'x'}, dimensions={0}, use_global_device_ids=true | all-gather | bytes 860160 | tf_op jit(solution)/shard_map/all_gather | solution.py:269
  72.7 1.7 %shard_map.91 = bf16[4,400,384]{2,1,0:T(8,128)(2,1)S(1)} custom-call(bf16[384,896]{1,0:T(8,128)(2,1)S(1)} %all_gather.23.d_ref, bf16[384,1536]{1,0:T(8,128)(2,1)S(1)} %bitcast.11, bf16[384,1536]{1,0:T(8,128)(2,1)S(1)} %bitcast.14), custom_call_target="tpu_custom_call" | custom-call | flops 905969664 | bytes 4276224 | tf_op jit(solution)/shard_map/pallas_call | solution.py:40
  74.4 18.2 %all_to_all.21.part_ref = bf16[4,400,384]{2,1,0:T(8,128)(2,1)S(1)} all-to-all(bf16[4,400,384]{2,1,0:T(8,128)(2,1)S(1)} %shard_map.91), channel_id=1, replica_groups=mesh['zl'=4,'c'=2,'y'=4,'zh'=4,'x'=4] {'y'}, dimensions={0} | all-to-all | bytes 2457600 | tf_op jit(solution)/shard_map/all_to_all | solution.py:217
  92.6 0.2 shard_map.92
  92.8 13.9 %all_to_all.22.back_ref = bf16[8,56,384]{2,1,0:T(8,128)(2,1)S(1)} all-to-all(bf16[8,56,384]{2,1,0:T(8,128)(2,1)S(1)} %shard_map.92), channel_id=1, replica_groups=mesh['zl'=4,'c'=2,'y'=4,'zh'=4,'x'=4] {'zl','c'}, dimensions={0} | all-to-all | bytes 688128 | tf_op jit(solution)/shard_map/all_to_all | solution.py:217
  106.7 0.4 shard_map.93
  107.0 26.3 %all-gather.1 = bf16[576,384]{1,0:T(8,128)(2,1)S(1)} all-gather(bf16[144,384]{1,0:T(8,128)(2,1)S(1)} %shard_map.93), channel_id=3, replica_groups=mesh['zl'=4,'c'=2,'y'=4,'zh'=4,'x'=4] {'zh'}, dimensions={0}, use_global_device_ids=true | all-gather | bytes 552960 | tf_op jit(solution)/shard_map/all_gather | solution.py:288
  133.4 0.1 shard_map.94
  133.4 12.9 %all-gather.2 = bf16[512,384]{1,0:T(8,128)(2,1)S(1)} all-gather(bf16[128,384]{1,0:T(8,128)(2,1)S(1)} %shard_map.94), channel_id=4, replica_groups=mesh['zl'=4,'c'=2,'y'=4,'zh'=4,'x'=4] {'y'}, dimensions={0}, use_global_device_ids=true | all-gather | bytes 491520 | tf_op jit(solution)/shard_map/all_gather | solution.py:293
  146.3 0.8 shard_map.95
  (14 shorter events, 0.0 us)
Async XLA Ops:
  0.6 1.4 copy-start.5
  0.6 33.1 %copy-start.1 = (bf16[1,384,1536]{2,1,0:T(8,128)(2,1)S(1)}, bf16[1,384,1536]{2,1,0:T(8,128)(2,1)}, u32[]{:S(2)}) copy-start(bf16[1,384,1536]{2,1,0:T(8,128)(2,1)} %param.12) | copy-start | bytes 3538948
  0.7 33.1 %copy-start.3 = (bf16[1,384,1536]{2,1,0:T(8,128)(2,1)S(1)}, bf16[1,384,1536]{2,1,0:T(8,128)(2,1)}, u32[]{:S(2)}) copy-start(bf16[1,384,1536]{2,1,0:T(8,128)(2,1)} %param.13) | copy-start | bytes 3538948
  2.0 31.8 %copy-start = (bf16[1,384,1536]{2,1,0:T(8,128)(2,1)S(1)}, bf16[1,384,1536]{2,1,0:T(8,128)(2,1)}, u32[]{:S(2)}) copy-start(bf16[1,384,1536]{2,1,0:T(8,128)(2,1)} %param.11) | copy-start | bytes 3538948
  3.7 22.1 %collective-permute-start = (bf16[2,48,1536]{2,1,0:T(8,128)(2,1)S(1)}, bf16[2,48,1536]{2,1,0:T(8,128)(2,1)S(1)}, u32[]{:S(2)}, u32[]{:S(2)}) collective-permute-start(bf16[2,48,1536]{2,1,0:T(8,128)(2,1)S(1)} %get-tuple-element.12), channel_id=1, source_target_pairs={{0,128},{64,192},{128,256},{192,320},{256,384},{320,448},{384,4},{... | collective-permute-start | bytes 884744 | tf_op jit(solution)/shard_map/ppermute | solution.py:248
  7.5 26.3 %collective-permute-start.1 = (bf16[2,48,1536]{2,1,0:T(8,128)(2,1)S(1)}, bf16[2,48,1536]{2,1,0:T(8,128)(2,1)S(1)}, u32[]{:S(2)}, u32[]{:S(2)}) collective-permute-start(bf16[2,48,1536]{2,1,0:T(8,128)(2,1)S(1)} %get-tuple-element.13), channel_id=1, source_target_pairs={{0,396},{64,460},{128,0},{192,64},{256,128},{320,192},{384,256},{4... | collective-permute-start | bytes 884744 | tf_op jit(solution)/shard_map/ppermute | solution.py:248
  17.0 16.7 %collective-permute-start.2 = (bf16[2,48,1536]{2,1,0:T(8,128)(2,1)S(1)}, bf16[2,48,1536]{2,1,0:T(8,128)(2,1)S(1)}, u32[]{:S(2)}, u32[]{:S(2)}) collective-permute-start(bf16[2,48,1536]{2,1,0:T(8,128)(2,1)S(1)} %get-tuple-element.14), channel_id=1, source_target_pairs={{0,192},{64,128},{128,320},{192,256},{256,448},{320,384},{384,68},... | collective-permute-start | bytes 884744 | tf_op jit(solution)/shard_map/ppermute | solution.py:248
  18.9 14.8 %collective-permute-start.3 = (bf16[2,48,1536]{2,1,0:T(8,128)(2,1)S(1)}, bf16[2,48,1536]{2,1,0:T(8,128)(2,1)S(1)}, u32[]{:S(2)}, u32[]{:S(2)}) collective-permute-start(bf16[2,48,1536]{2,1,0:T(8,128)(2,1)S(1)} %get-tuple-element.15), channel_id=1, source_target_pairs={{0,460},{64,396},{128,64},{192,0},{256,192},{320,128},{384,320},{4... | collective-permute-start | bytes 884744 | tf_op jit(solution)/shard_map/ppermute | solution.py:248
  23.8 17.2 %collective-permute-start.4 = (bf16[2,48,1536]{2,1,0:T(8,128)(2,1)}, bf16[2,48,1536]{2,1,0:T(8,128)(2,1)}, u32[]{:S(2)}, u32[]{:S(2)}) collective-permute-start(bf16[2,48,1536]{2,1,0:T(8,128)(2,1)} %get-tuple-element.16), channel_id=1, source_target_pairs={{0,256},{64,320},{128,384},{192,448},{256,4},{320,68},{384,132},{4... | collective-permute-start | bytes 884744 | tf_op jit(solution)/shard_map/ppermute | solution.py:248
  25.7 16.3 %collective-permute-start.5 = (bf16[2,48,1536]{2,1,0:T(8,128)(2,1)S(1)}, bf16[2,48,1536]{2,1,0:T(8,128)(2,1)}, u32[]{:S(2)}, u32[]{:S(2)}) collective-permute-start(bf16[2,48,1536]{2,1,0:T(8,128)(2,1)S(1)} %get-tuple-element.17), channel_id=1, source_target_pairs={{0,332},{64,268},{128,460},{192,396},{256,64},{320,0},{384,192},{4... | collective-permute-start | bytes 884744 | tf_op jit(solution)/shard_map/ppermute | solution.py:248
  35.3 0.9 copy-start.2
  36.2 13.3 %all-to-all-start = ((bf16[4,72,1152]{2,1,0:T(8,128)(2,1)}), bf16[4,72,1152]{2,1,0:T(8,128)(2,1)S(1)}, u32[]{:S(2)}, u32[]{:S(2)}) async-start(bf16[4,72,1152]{2,1,0:T(8,128)(2,1)} %bitcast.17), calls=%async_computation | async-start | bytes 1327104 | tf_op jit(solution)/shard_map/all_to_all | solution.py:217
  42.0 1.3 copy-start.4
  92.6 14.1 %copy-start.6 = (bf16[8,48]{1,0:T(8,128)(2,1)S(1)}, bf16[8,48]{1,0:T(8,128)(2,1)}, u32[]{:S(2)}) copy-start(bf16[8,48]{1,0:T(8,128)(2,1)} %weights_ref.1) | copy-start | bytes 2308
